TPU v7x, 128 devices: a whole 4x4x4 slice. The times are simulated.
128 devices in a mesh: row: 8 (over y, core), col: 16 (over x, z).
Axes of the slice: x: 4, y: 4, z: 4, core: 2. Of those that a mesh axis runs over, the one named last changes fastest.
Arguments:
- tokens: bfloat16 [1024, 16384], P('col', 'row'), may hold values from -6 to 6
- segment_ids: int32 [1024], replicated, may hold values from 0 to 3, never falling along the last dimension, each value on 1 to 512 neighbouring positions
- w_query: bfloat16 [16384, 16384], P('row', 'col'), may hold values from -8 to 8
- w_key: bfloat16 [16384, 1024], P('row', 'col'), may hold values from -8 to 8
- value_weight: bfloat16 [16384, 1024], P('row', 'col'), may hold values from -0.046875 to 0.046875
- w_out: bfloat16 [16384, 16384], P('col', 'row'), may hold values from -0.046875 to 0.046875
- grad_out: bfloat16 [1024, 16384], P('col', 'row'), may hold values from -6 to 6
Outputs:
- mixed: bfloat16 [1024, 16384], P('col', 'row')
- grad_tokens: bfloat16 [1024, 16384], P('col', 'row')
- grad_w_query: bfloat16 [16384, 16384], P('row', 'col')
- grad_w_key: bfloat16 [16384, 1024], P('row', 'col')
- grad_w_value: bfloat16 [16384, 1024], P('row', 'col')
- grad_w_out: bfloat16 [16384, 16384], P('col', 'row')
Inputs may be any that keep to these rules, and one draw needn't show every extreme that they name: `segment_ids`: document ids never fall along the tokens; each document holds 1 to 512 tokens, and one holds exactly 512.
All inputs are finite; a program needn't handle non-finite values.
Results may differ from a plain program's by a relative error of at most 0.04.
The roundings to bfloat16 on the way count: a program that leaves them out, or rounds other values in their place, can miss the bound.
Values may be sent and summed in bfloat16 or wider, within the bound.
A program may use at most 128 MiB of HBM per device.

v0:
```python
import jax
import jax.numpy as jnp
from jax import lax
from jax.sharding import PartitionSpec as P

KEY_VALUE_HEADS = 8
HEAD_SIZE = 128


def swapped(value, axis, bit):
    mask = 2**bit
    pairs = [(source, source ^ mask) for source in range(lax.axis_size(axis))]
    return lax.ppermute(value, axis, pairs)


def attention_probs(query_matrix, keys_block, allowed, scale):
    scores = (
        jnp.einsum("rgd,sd->grs", query_matrix.astype(jnp.float32), keys_block.astype(jnp.float32))
        * scale
    )
    scores = jnp.where(allowed[None] > 0, scores, jnp.float32(-1e30))
    highest = jnp.max(scores, axis=-1, keepdims=True)
    expo = jnp.exp(scores - highest)
    return expo / jnp.sum(expo, axis=-1, keepdims=True)


def forward_group(query_matrix, keys_block, values_block, allowed, scale):
    probs = attention_probs(query_matrix, keys_block, allowed, scale)
    probs_low = probs.astype(jnp.bfloat16)
    result = jnp.einsum("grs,sd->rgd", probs_low, values_block, preferred_element_type=jnp.float32)
    return result.astype(jnp.bfloat16)


def backward_group(query_matrix, keys_block, values_block, grad_heads, allowed, scale):
    probs = attention_probs(query_matrix, keys_block, allowed, scale)
    probs_low = probs.astype(jnp.bfloat16)
    grad_probs = jnp.einsum(
        "rgd,sd->grs", grad_heads, values_block, preferred_element_type=jnp.float32
    )
    inner = jnp.sum(probs * grad_probs, axis=-1, keepdims=True)
    grad_scores = (probs * (grad_probs - inner) * scale).astype(jnp.bfloat16)
    grad_q = jnp.einsum(
        "grs,sd->rgd", grad_scores, keys_block, preferred_element_type=jnp.float32
    ).astype(jnp.bfloat16)
    key_gradient_rows = jnp.einsum(
        "grs,rgd->sd", grad_scores, query_matrix, preferred_element_type=jnp.float32
    )
    value_gradient_rows = jnp.einsum(
        "grs,rgd->sd", probs_low, grad_heads, preferred_element_type=jnp.float32
    )
    return (grad_q, key_gradient_rows, value_gradient_rows)


def contract_last(left, right):
    return lax.dot_general(
        left, right, (((1,), (1,)), ((), ())), preferred_element_type=jnp.float32
    )


def contract_first(left, right):
    return lax.dot_general(
        left, right, (((0,), (0,)), ((), ())), preferred_element_type=jnp.float32
    )


def gather_cols(panel):
    return lax.all_gather(panel, "col", axis=0, tiled=True)


def gather_rows(panel):
    return lax.all_gather(panel, "row", axis=0, tiled=True)


def reduce_rows(term_fn, rows_here):
    return lax.psum_scatter(
        term_fn(jnp.int32(0), rows_here * lax.axis_size("row")),
        "row",
        scatter_dimension=0,
        tiled=True,
    )


def reduce_cols(term_fn, rows_here):
    return lax.psum_scatter(
        term_fn(jnp.int32(0), lax.axis_size("col") * rows_here).astype(jnp.bfloat16),
        "col",
        scatter_dimension=0,
        tiled=True,
    ).astype(jnp.float32)


def partner(piece, bit_index):
    return swapped(piece.astype(jnp.bfloat16), "col", bit_index).astype(piece.dtype)


def span_bits():
    return (lax.axis_size("col") // KEY_VALUE_HEADS).bit_length() - 1


def join_pairs(piece):
    col_index = lax.axis_index("col")
    other = partner(piece, 0)
    is_low = col_index // 2**0 % 2 == 0
    piece = jnp.where(
        is_low, jnp.concatenate([piece, other], axis=-1), jnp.concatenate([other, piece], axis=-1)
    )
    return piece


def split_pairs(piece):
    col_index = lax.axis_index("col")
    for bit_index in reversed(range(span_bits())):
        half_width = piece.shape[-1] // 2
        lower = piece[..., :half_width]
        upper = piece[..., half_width:]
        is_low = col_index // 2**bit_index % 2 == 0
        keep = jnp.where(is_low, lower, upper)
        outgoing = jnp.where(is_low, upper, lower)
        piece = keep + partner(outgoing, bit_index)
    return piece


def shards(tokens, segment_ids, w_query, w_key, value_weight, w_out, grad_out):
    row_devices = lax.axis_size("row")
    col_devices = lax.axis_size("col")
    scale = HEAD_SIZE ** (-0.5)
    tokens_full = gather_cols(tokens)
    sequence_length = tokens_full.shape[0]
    local_rows = sequence_length // row_devices
    out_rows = sequence_length // col_devices
    query_width = w_query.shape[1]
    key_width = w_key.shape[1]
    heads_here = query_width // HEAD_SIZE
    weights_in = jnp.concatenate([w_query, w_key, value_weight], axis=1)

    def project_rows(first_row, row_total):
        return jnp.dot(tokens_full, weights_in, preferred_element_type=jnp.float32)

    projected = reduce_rows(project_rows, local_rows)
    query_rows = projected[:, :query_width].astype(jnp.bfloat16)
    pair_part = projected[:, query_width:].reshape(local_rows, 2, key_width)
    kv_all = gather_rows(join_pairs(pair_part).astype(jnp.bfloat16))
    every_key = kv_all[:, 0, :]
    every_value = kv_all[:, 1, :]
    row_first = lax.axis_index("row") * local_rows
    positions = jnp.arange(sequence_length, dtype=jnp.int32)
    query_pos = row_first + jnp.arange(local_rows, dtype=jnp.int32)
    segment_rows = lax.dynamic_slice_in_dim(segment_ids, row_first, local_rows, 0)
    allowed = (
        (segment_rows[:, None] == segment_ids[None, :]) & (positions[None, :] <= query_pos[:, None])
    ).astype(jnp.int32)
    query_matrix = query_rows.reshape(local_rows, heads_here, HEAD_SIZE)
    attended = forward_group(query_matrix, every_key, every_value, allowed, scale).reshape(
        local_rows, query_width
    )
    attended_full = gather_rows(attended)

    def output_rows(first_row, row_total):
        return jnp.dot(attended_full, w_out, preferred_element_type=jnp.float32)

    mixed = reduce_cols(output_rows, out_rows).astype(jnp.bfloat16)
    grad_full = gather_cols(grad_out)
    grad_w_out = contract_first(attended_full, grad_full).astype(jnp.bfloat16)

    def attended_grad_rows(first_row, row_total):
        return contract_last(grad_full, w_out)

    attended_gradient = reduce_rows(attended_grad_rows, local_rows).astype(jnp.bfloat16)
    grad_heads = attended_gradient.reshape(local_rows, heads_here, HEAD_SIZE)
    grad_q, key_gradient_rows, value_gradient_rows = backward_group(
        query_matrix, every_key, every_value, grad_heads, allowed, scale
    )
    partial_kv = jnp.stack([key_gradient_rows, value_gradient_rows], axis=1)
    flat_partial = partial_kv.reshape(sequence_length, 2 * HEAD_SIZE)

    def partial_rows(first_row, row_total):
        return flat_partial

    summed = reduce_rows(partial_rows, local_rows).reshape(local_rows, 2, HEAD_SIZE)
    grad_kv = split_pairs(summed)
    grad_kv_low = grad_kv.reshape(local_rows, 2 * key_width).astype(jnp.bfloat16)
    grad_local = jnp.concatenate([grad_q.reshape(local_rows, query_width), grad_kv_low], axis=1)
    grad_all = gather_rows(grad_local)

    def input_grad_rows(first_row, row_total):
        return contract_last(grad_all, weights_in)

    grad_tokens = reduce_cols(input_grad_rows, out_rows).astype(jnp.bfloat16)
    grad_weights = contract_first(tokens_full, grad_all).astype(jnp.bfloat16)
    grad_w_query = grad_weights[:, :query_width]
    grad_w_key = grad_weights[:, query_width : query_width + key_width]
    grad_w_value = grad_weights[:, query_width + key_width :]
    return (mixed, grad_tokens, grad_w_query, grad_w_key, grad_w_value, grad_w_out)


def solution(mesh):
    placed = (
        P("col", "row"),
        P(),
        P("row", "col"),
        P("row", "col"),
        P("row", "col"),
        P("col", "row"),
        P("col", "row"),
    )
    return jax.shard_map(
        shards,
        mesh=mesh,
        in_specs=placed,
        out_specs=(
            P("col", "row"),
            P("col", "row"),
            P("row", "col"),
            P("row", "col"),
            P("row", "col"),
            P("col", "row"),
        ),
        check_vma=False,
    )
```

profile of v0, /device:TPU:0, one launch (start us, length us, event | category | flops | bytes accessed | tf_op | source)
XLA Modules:
  0.0 494.3 jit_solution(4338528273361062160)
XLA Ops:
  7.2 0.0 all-gather.5.cloned.1.call-start
  7.2 0.7 all-gather.5.cloned.1.call-update
  7.9 0.0 all-gather.9.cloned.1.call-start
  7.9 0.7 all-gather.9.cloned.1.call-update
  8.7 0.0 reduce-scatter.6.cloned.1.call-start
  8.7 1.2 copy.28
  9.9 1.2 copy.29
  11.2 7.9 %concatenate.12 = bf16[2048,1152]{1,0:T(8,128)(2,1)} concatenate(bf16[2048,1024]{1,0:T(8,128)(2,1)} %param.9, bf16[2048,64]{1,0:T(8,128)(2,1)S(1)} %copy.28, bf16[2048,64]{1,0:T(8,128)(2,1)S(1)} %copy.29), dimensions={1} | concatenate | bytes 9437184 | tf_op jit(solution)/shard_map/concatenate | solution.py:134
  19.0 45.3 %all-gather.5.cloned.1.call-done = bf16[1024,2048]{1,0:T(8,128)(2,1)} async-done(((bf16[64,2048]{1,0:T(8,128)(2,1)}), bf16[1024,2048]{1,0:T(8,128)(2,1)}) %all-gather.5.cloned.1.call-update) | async-done | bytes 4194320 | tf_op jit(solution)/shard_map/all_gather | solution.py:67
  64.3 9.8 %convolution_bitcast_fusion = f32[1024,1152]{0,1:T(8,128)} fusion(bf16[2048,1152]{1,0:T(8,128)(2,1)} %concatenate.12, bf16[1024,2048]{1,0:T(8,128)(2,1)} %all-gather.5.cloned.1.call-done), kind=kOutput, calls=%fused_computation.4 | convolution fusion | flops 4831838208 | bytes 13631488 | tf_op jit(solution)/shard_map/dot_general | solution.py:137
  74.1 0.0 reduce-scatter.6.cloned.1.call-update
  74.1 0.0 reduce-scatter.10.cloned.1.call-start
  74.1 43.6 %all-gather.9.cloned.1.call-done = bf16[1024,2048]{1,0:T(8,128)(2,1)} async-done(((bf16[64,2048]{1,0:T(8,128)(2,1)}), bf16[1024,2048]{1,0:T(8,128)(2,1)}) %all-gather.9.cloned.1.call-update) | async-done | bytes 4194320 | tf_op jit(solution)/shard_map/all_gather | solution.py:67
  117.7 10.0 %fusion.31 = f32[1024,1024]{1,0:T(8,128)} fusion(bf16[1024,2048]{1,0:T(8,128)(2,1)} %all-gather.9.cloned.1.call-done, bf16[1024,2048]{1,0:T(8,128)(2,1)} %param.12), kind=kOutput, calls=%fused_computation.53 | convolution fusion | flops 4294967296 | bytes 12582912 | tf_op jit(solution)/shard_map/dot_general | solution.py:55
  127.7 0.0 reduce-scatter.10.cloned.1.call-update
  127.7 0.0 reduce-scatter.12.cloned.1.call-start
  127.8 0.6 copy-done.2
  128.4 0.1 dynamic_slice.3
  128.5 30.2 %reduce-scatter.6.cloned.1.call-done = f32[128,1152]{0,1:T(8,128)} async-done(((f32[1024,1152]{0,1:T(8,128)}), f32[128,1152]{0,1:T(8,128)}) %reduce-scatter.6.cloned.1.call-update) | async-done | bytes 589840 | tf_op jit(solution)/shard_map/reduce_scatter | solution.py:75
  158.7 0.8 slice.37
  159.5 1.7 collective-permute-start
  161.2 0.2 convert_compare_fusion
  161.5 37.1 %reduce-scatter.10.cloned.1.call-done = f32[128,1024]{1,0:T(8,128)} async-done(((f32[1024,1024]{1,0:T(8,128)}), f32[128,1024]{1,0:T(8,128)}) %reduce-scatter.10.cloned.1.call-update) | async-done | bytes 524304 | tf_op jit(solution)/shard_map/reduce_scatter | solution.py:75
  198.6 1.1 convert_element_type.82
  199.7 0.2 copy.49
  199.8 1.1 slice.62
  200.9 0.0 collective-permute-done
  201.0 12.2 %all_gather.16 = bf16[1024,2,128]{0,2,1:T(8,128)(2,1)S(1)} all-gather(bf16[128,2,128]{0,2,1:T(8,128)(2,1)S(1)} %fusion.22), channel_id=1, replica_groups=mesh['row'=8,'col'=16] {'row'}, dimensions={0}, use_global_device_ids=true | all-gather | bytes 589824 | tf_op jit(solution)/shard_map/all_gather | solution.py:71
  213.2 2.7 fusion.20
  215.9 3.5 fusion.30
  219.4 3.0 convolution_bitcast_fusion.1
  222.4 7.4 %fusion.13 = f32[1024,1,128]{0,2,1:T(8,128)S(1)} fusion(bf16[128,8,128]{0,2,1:T(8,128)(2,1)S(1)} %bitcast.108, f32[1024,128,8]{1,0,2:T(8,128)} %fusion.20, f32[8,128,1024]{1,2,0:T(8,128)} %get-tuple-element.21, f32[8,128]{1,0:T(8,128)S(1)} %get-tuple-element.20), kind=kOutput, calls=%fused_computation.23 | convolution fusion | flops 275777536 | bytes 9179136 | tf_op jit(solution)/shard_map/grs,rgd->sd/dot_general | solution.py:45
  229.8 1.0 pad_maximum_fusion
  230.9 0.0 reduce-scatter.12.cloned.1.call-update
  230.9 0.2 all-gather.7.cloned.1.call-start
  231.1 3.3 convolution_convert_fusion.4
  234.5 0.0 all-gather.7.cloned.1.call-update
  234.5 0.0 all-gather.11.cloned.1.call-start
  234.6 29.4 %reduce-scatter.12.cloned.1.call-done = f32[128,256]{0,1:T(8,128)} async-done(((f32[1024,256]{0,1:T(8,128)}), f32[128,256]{0,1:T(8,128)}) %reduce-scatter.12.cloned.1.call-update) | async-done | bytes 131088 | tf_op jit(solution)/shard_map/reduce_scatter | solution.py:75
  263.9 0.9 select_convert_fusion
  264.8 0.0 copy-start.1
  264.8 1.6 collective-permute-start.1
  266.4 7.3 %fusion.14 = bf16[128,8,128]{2,0,1:T(8,128)(2,1)S(1)} fusion(f32[1024,128,8]{1,0,2:T(8,128)} %fusion.20, bf16[1024,2,128]{0,2,1:T(8,128)(2,1)S(1)} %all_gather.16, f32[8,128,1024]{1,2,0:T(8,128)} %get-tuple-element.21, f32[8,128]{1,0:T(8,128)S(1)} %get-tuple-element.20), kind=kOutput, calls=%fused_computation.25 | convolution fusion | flops 275908608 | bytes 17309696 | tf_op jit(solution)/shard_map/grs,sd->rgd/dot_general | solution.py:42
  273.7 0.0 collective-permute-done.1
  273.7 0.7 pad_maximum_fusion.1
  274.5 0.0 all-gather.11.cloned.1.call-update
  274.5 0.0 reduce-scatter.8.cloned.1.call-start
  274.6 17.6 %all-gather.7.cloned.1.call-done = bf16[1024,1024]{0,1:T(8,128)(2,1)} async-done(((bf16[128,1024]{0,1:T(8,128)(2,1)}), bf16[1024,1024]{0,1:T(8,128)(2,1)}) %all-gather.7.cloned.1.call-update) | async-done | bytes 2097168 | tf_op jit(solution)/shard_map/all_gather | solution.py:71
  292.1 9.3 %convolution_convert_fusion.3 = bf16[1024,2048]{1,0:T(8,128)(2,1)} fusion(bf16[1024,1024]{0,1:T(8,128)(2,1)} %all-gather.7.cloned.1.call-done, bf16[1024,2048]{1,0:T(8,128)(2,1)} %param.12), kind=kOutput, calls=%fused_computation.14 | convolution fusion | flops 4297064448 | bytes 10485760 | tf_op jit(solution)/shard_map/dot_general | solution.py:159
  301.5 0.0 reduce-scatter.8.cloned.1.call-update
  301.5 0.3 reduce-scatter.14.cloned.1.call-start
  301.7 22.0 %all-gather.11.cloned.1.call-done = bf16[1024,1152]{0,1:T(8,128)(2,1)} async-done(((bf16[128,1152]{0,1:T(8,128)(2,1)}), bf16[1024,1152]{0,1:T(8,128)(2,1)}) %all-gather.11.cloned.1.call-update) | async-done | bytes 2359312 | tf_op jit(solution)/shard_map/all_gather | solution.py:71
  323.7 9.6 %convolution_convert_fusion.1 = bf16[1024,2048]{1,0:T(8,128)(2,1)} fusion(bf16[1024,1152]{0,1:T(8,128)(2,1)} %all-gather.11.cloned.1.call-done, bf16[2048,1152]{1,0:T(8,128)(2,1)} %concatenate.12), kind=kOutput, calls=%fused_computation.12 | convolution fusion | flops 4833935360 | bytes 11272192 | tf_op jit(solution)/shard_map/dot_general | solution.py:55
  333.4 0.0 reduce-scatter.14.cloned.1.call-update
  333.4 1.6 copy-done.5
  335.0 8.3 %convolution_convert_fusion.2 = bf16[1024,2048]{1,0:T(8,128)(2,1)} fusion(bf16[1024,1024]{0,1:T(8,128)(2,1)S(1)} %copy-done.5, bf16[1024,2048]{1,0:T(8,128)(2,1)} %all-gather.9.cloned.1.call-done), kind=kOutput, calls=%fused_computation.13 | convolution fusion | flops 4297064448 | bytes 10485760 | tf_op jit(solution)/shard_map/dot_general | solution.py:61
  343.3 0.0 copy-done.4
  343.3 5.3 %fusion.2 = bf16[2048,1152]{0,1:T(8,128)(2,1)S(1)} fusion(bf16[1024,1152]{0,1:T(8,128)(2,1)S(1)} %copy-done.4, bf16[1024,2048]{1,0:T(8,128)(2,1)S(1)} %copy-done.3), kind=kOutput, calls=%fused_computation.3 | convolution fusion | flops 4834197504 | bytes 11272192 | tf_op jit(solution)/shard_map/dot_general | solution.py:61
  348.7 2.1 copy-done
  350.8 2.3 slice.43
  353.1 6.4 %copy.39 = bf16[2048,1024]{1,0:T(8,128)(2,1)} copy(bf16[2048,1024]{0,1:T(8,128)(2,1)} %slice.43) | data formatting | bytes 8388608
  359.5 1.9 fusion.29
  361.4 45.1 %reduce-scatter.8.cloned.1.call-done = bf16[64,2048]{1,0:T(8,128)(2,1)} async-done(((bf16[1024,2048]{1,0:T(8,128)(2,1)}), bf16[64,2048]{1,0:T(8,128)(2,1)}) %reduce-scatter.8.cloned.1.call-update) | async-done | bytes 262160 | tf_op jit(solution)/shard_map/reduce_scatter | solution.py:84
  406.5 81.3 %reduce-scatter.14.cloned.1.call-done = bf16[64,2048]{1,0:T(8,128)(2,1)} async-done(((bf16[1024,2048]{1,0:T(8,128)(2,1)}), bf16[64,2048]{1,0:T(8,128)(2,1)}) %reduce-scatter.14.cloned.1.call-update) | async-done | bytes 262160 | tf_op jit(solution)/shard_map/reduce_scatter | solution.py:84
  (10 shorter events, 0.0 us)
Async XLA Ops:
  7.2 57.1 %all-gather.5.cloned.1.call-start = ((), (), s32[]{:S(2)}) async-start(), calls=%async_computation.5 | async-start | bytes 4456448 | tf_op jit(solution)/shard_map/all_gather | solution.py:67
  7.9 109.8 %all-gather.9.cloned.1.call-start = ((), (), s32[]{:S(2)}) async-start(), calls=%async_computation.9 | async-start | bytes 4456448 | tf_op jit(solution)/shard_map/all_gather | solution.py:67
  8.7 150.1 %reduce-scatter.6.cloned.1.call-start = ((), (), s32[]{:S(2)}) async-start(), calls=%async_computation.6 | async-start | bytes 5308416 | tf_op jit(solution)/shard_map/reduce_scatter | solution.py:75
  74.1 124.5 %reduce-scatter.10.cloned.1.call-start = ((), (), s32[]{:S(2)}) async-start(), calls=%async_computation.10 | async-start | bytes 4718592 | tf_op jit(solution)/shard_map/reduce_scatter | solution.py:75
  127.7 0.7 copy-start.2
  127.7 136.2 %reduce-scatter.12.cloned.1.call-start = ((), (), s32[]{:S(2)}) async-start(), calls=%async_computation.11 | async-start | bytes 1179648 | tf_op jit(solution)/shard_map/reduce_scatter | solution.py:75
  159.5 41.4 %collective-permute-start = (bf16[128,2,64]{0,2,1:T(8,128)(2,1)S(1)}, bf16[128,2,64]{0,2,1:T(8,128)(2,1)S(1)}, u32[]{:S(2)}, u32[]{:S(2)}) collective-permute-start(bf16[128,2,64]{0,2,1:T(8,128)(2,1)S(1)} %bitcast.111), channel_id=1, source_target_pairs={{0,1},{1,0},{2,3},{3,2},{4,5},{5,4},{6,7},{7,6},{8,9},{9,8},{10,11... | collective-permute-start | bytes 98312 | tf_op jit(solution)/shard_map/ppermute | solution.py:13
  230.9 61.2 %all-gather.7.cloned.1.call-start = ((), (), s32[]{:S(2)}) async-start(), calls=%async_computation.7 | async-start | bytes 2359296 | tf_op jit(solution)/shard_map/all_gather | solution.py:71
  234.5 89.2 %all-gather.11.cloned.1.call-start = ((), (), s32[]{:S(2)}) async-start(), calls=%async_computation.12 | async-start | bytes 2654208 | tf_op jit(solution)/shard_map/all_gather | solution.py:71
  264.8 8.9 %copy-start.1 = (f32[128,256]{0,1:T(8,128)S(1)}, f32[128,256]{0,1:T(8,128)}, u32[]{:S(2)}) copy-start(f32[128,256]{0,1:T(8,128)} %reduce-scatter.12.cloned.1.call-done) | copy-start | bytes 393220
  264.8 8.9 %collective-permute-start.1 = (bf16[128,2,64]{0,2,1:T(8,128)(2,1)S(1)}, bf16[128,2,64]{0,2,1:T(8,128)(2,1)S(1)}, u32[]{:S(2)}, u32[]{:S(2)}) collective-permute-start(bf16[128,2,64]{0,2,1:T(8,128)(2,1)S(1)} %select_convert_fusion), channel_id=1, source_target_pairs={{0,1},{1,0},{2,3},{3,2},{4,5},{5,4},{6,7},{7,6},{8,9},{9,8},{10,11... | collective-permute-start | bytes 98312 | tf_op jit(solution)/shard_map/ppermute | solution.py:13
  274.5 132.0 %reduce-scatter.8.cloned.1.call-start = ((), (), s32[]{:S(2)}) async-start(), calls=%async_computation.8 | async-start | bytes 4456448 | tf_op jit(solution)/shard_map/reduce_scatter | solution.py:84
  301.5 186.3 %reduce-scatter.14.cloned.1.call-start = ((), (), s32[]{:S(2)}) async-start(), calls=%async_computation.13 | async-start | bytes 4456448 | tf_op jit(solution)/shard_map/reduce_scatter | solution.py:84
  333.4 1.6 copy-start.5
  335.0 8.3 %copy-start.3 = (bf16[1024,2048]{1,0:T(8,128)(2,1)S(1)}, bf16[1024,2048]{1,0:T(8,128)(2,1)}, u32[]{:S(2)}) copy-start(bf16[1024,2048]{1,0:T(8,128)(2,1)} %all-gather.5.cloned.1.call-done) | copy-start | bytes 12582916
  335.0 8.3 %copy-start.4 = (bf16[1024,1152]{0,1:T(8,128)(2,1)S(1)}, bf16[1024,1152]{0,1:T(8,128)(2,1)}, u32[]{:S(2)}) copy-start(bf16[1024,1152]{0,1:T(8,128)(2,1)} %all-gather.11.cloned.1.call-done) | copy-start | bytes 7077892
  348.6 2.1 copy-start
Sparse Core Ops, SparseCore 0:
  10.1 54.1 all-gather.4
  66.4 51.2 all-gather.8
  120.1 38.5 reduce-scatter.5
  161.5 37.0 reduce-scatter.9
  231.0 32.8 reduce-scatter.11
  266.0 26.0 all-gather.6
  294.4 29.3 all-gather.10
  327.6 78.7 reduce-scatter.7
  410.7 77.0 reduce-scatter.13
where the time goes:
time: 495 us; the launch traced here: 494 us
  waiting for transfers between devices  353 us (71%)
  matrix products  79.7 us (16%)
  local copies, waits for them, and re-layouts  27.4 us (6%)
  between operations  14 us (3%)
  blocking collectives  12.2 us (2%)
    reduce_scatter x2, waiting for transfers between devices, reduce_cols(): lax.psum_scatter(term_fn(jnp.int32(0), lax.axis_size('col') * rows_here)....  126 us
    reduce_scatter x3, waiting for transfers between devices, reduce_rows(): lax.psum_scatter(term_fn(jnp.int32(0), rows_here * lax.axis_size('row')),...  96.7 us
    all_gather x2, waiting for transfers between devices, gather_cols(): return lax.all_gather(panel, 'col', axis=0, tiled=True)  88.8 us
    all_gather x2, waiting for transfers between devices, gather_rows(): return lax.all_gather(panel, 'row', axis=0, tiled=True)  39.6 us
    dot_general x2, matrix products, contract_last(): lax.dot_general(left, right, (((1,), (1,)), ((), ())), preferred_element_...  19.6 us
    dot_general x2, matrix products, contract_first(): lax.dot_general(left, right, (((0,), (0,)), ((), ())), preferred_element_...  13.7 us
    unnamed x15, local copies, waits for them, and re-layouts  13.2 us
    all_gather x1, blocking collectives, gather_rows(): return lax.all_gather(panel, 'row', axis=0, tiled=True)  12.2 us
  transfers between devices with their start and end apart: 11, of which 9 were waited for; matrix products, arithmetic and copies ran while one was open for 18% of the time, Pallas kernels for 0%

commit v1 on v0

v1 whole, which is shorter than its diff:
```python
import jax
import jax.numpy as jnp
from jax import lax
from jax.experimental import pallas as pl
from jax.experimental.pallas import tpu as pltpu
from jax.sharding import PartitionSpec as P

HEAD = 128
CHUNKS = 8
TILE = 256
MESH = pl.DeviceIdType.MESH
F32 = jnp.float32
BF16 = jnp.bfloat16


def nn(left, right):
    return jnp.dot(left, right, preferred_element_type=F32)


def nt(left, right):
    return lax.dot_general(left, right, (((1,), (1,)), ((), ())), preferred_element_type=F32)


def tn(left, right):
    return lax.dot_general(left, right, (((0,), (0,)), ((), ())), preferred_element_type=F32)


def ring(value, step):
    return lax.rem(value + (step + 4), 4)


class Copies:
    def __init__(self, send, recv):
        self.send, self.recv = send, recv
        self.made = {}
        self.sent = set()

    def start(self, key, src, dst, device):
        index = len(self.made)
        copy = pltpu.make_async_remote_copy(
            src_ref=src,
            dst_ref=dst,
            send_sem=self.send.at[index],
            recv_sem=self.recv.at[index],
            device_id=device,
            device_id_type=MESH,
        )
        copy.start()
        self.made[key] = copy

    def arrived(self, *keys):
        for key in keys:
            self.made[key].wait_recv()

    def left(self, *keys):
        for key in keys:
            if key not in self.sent:
                self.made[key].wait_send()
                self.sent.add(key)

    def finish(self):
        self.left(*list(self.made))


SEMS = 160
VMEM_LIMIT = 64 * 2**20


def kernel(
    tokens, grad_out, wq_in, wk_in, wv_in, wo_in, mrow, mcol,
    mixed, gtokens, gwq, gwk, gwv, gwo,
    tok, grd, wq, wk, wv, wkv, wo,
    pt, xt, r1t, r2t, pg, xg, r1g, r2g, pd, xd, r1d, r2d,
    qr, kvp, kvo, gh, kv, mask, probs, dkt, dvt, dsum, dout, dback,
    att, gq, gkv,
    stfar, stnear, own, f1, f2, n1, n2, pfar, pnear, outst,
    send, recv, local, out_sem,
):
    row, col = lax.axis_index("row"), lax.axis_index("col")
    y, core = row // 2, lax.rem(row, 2)
    x, z = col // 4, lax.rem(col, 4)
    width = tok.shape[-1]
    heads = qr.shape[-1] // HEAD
    hn = heads * HEAD
    scale = HEAD ** (-0.5)

    def at_x(step):
        return {"col": ring(x, step) * 4 + z}

    def at_z(step):
        return {"col": x * 4 + ring(z, step)}

    def at_y(step):
        return {"row": ring(y, step) * 2 + core}

    at_core = {"row": y * 2 + (1 - core)}
    odd = lax.rem(z, 2)
    at_partner = {"col": x * 4 + (z + 1 - 2 * odd)}

    loads = [
        pltpu.make_async_copy(wq_in, wq, local.at[0]),
        pltpu.make_async_copy(wk_in, wk, local.at[1]),
        pltpu.make_async_copy(wv_in, wv, local.at[2]),
        pltpu.make_async_copy(wo_in, wo, local.at[3]),
    ]
    half = 32
    own_copies = []
    for n, (src, buf) in enumerate(((tokens, tok), (grad_out, grd))):
        own_copies.append(
            [
                pltpu.make_async_copy(src.at[0:half], buf.at[0, z, x], local.at[4 + 2 * n]),
                pltpu.make_async_copy(src.at[half:], buf.at[1, x, z], local.at[5 + 2 * n]),
            ]
        )
    for pair in own_copies:
        for copy in pair:
            copy.start()
    for copy in loads:
        copy.start()

    barrier = pltpu.get_barrier_semaphore()
    for device in (at_x(1), at_x(-1), at_z(1), at_z(-1), at_y(1), at_y(-1), at_core):
        pl.semaphore_signal(barrier, inc=1, device_id=device, device_id_type=MESH)
    pl.semaphore_wait(barrier, 7)

    cp = Copies(send, recv)

    def axes(h):
        return ((at_x, x), (at_z, z)) if h == 0 else ((at_z, z), (at_x, x))

    def ag1(name, src, buf):
        for h in range(2):
            (first, f), (_, s) = axes(h)
            for d in (1, -1):
                cp.start((name, 1, h, d), src.at[h * half : (h + 1) * half], buf.at[h, s, f], first(d))

    def ag1b(name, buf):
        for h in range(2):
            (first, f), (_, s) = axes(h)
            cp.arrived((name, 1, h, 1), (name, 1, h, -1))
            for d, lo in ((1, 0), (-1, 16)):
                part = buf.at[h, s, ring(f, -d), lo : lo + 16]
                cp.start((name, 2, h, d), part, part, first(d))

    def ag2(name, buf):
        for h in range(2):
            _, (second, s) = axes(h)
            cp.arrived((name, 2, h, 1), (name, 2, h, -1))
            for d in (1, -1):
                cp.start((name, 3, h, d), buf.at[h, s], buf.at[h, s], second(d))

    def ag2b(name, buf):
        for h in range(2):
            _, (second, s) = axes(h)
            cp.arrived((name, 3, h, 1), (name, 3, h, -1))
            for d, lo in ((1, 0), (-1, 2)):
                part = buf.at[h, ring(s, -d), lo : lo + 2]
                cp.start((name, 4, h, d), part, part, second(d))

    def ag_end(name):
        for h in range(2):
            cp.arrived((name, 4, h, 1), (name, 4, h, -1))

    steps = (0, 1, -1, 2)
    pairs = [(ring(z, s), ring(x, s)) for s in steps]

    def load_pair(buf, p):
        bz, bx = pairs[p]
        return jnp.concatenate(
            [buf[0, bz].reshape(128, width), buf[1, bx].reshape(128, width)], axis=0
        )

    def put_partial(dst, p, value, columns):
        size = value.shape[-1]
        five = value.reshape(2, 2, 4, 16, size)
        for h in range(2):
            for c in range(2):
                dst[c, 2 * p + h, :, :, columns] = five[h, c]

    def project(p):
        def body(n, carry):
            cols = pl.ds(pl.multiple_of(n * TILE, TILE), TILE)
            put_partial(pt, p, nn(load_pair(tok, p), wq[:, cols]), cols)
            return carry

        lax.fori_loop(0, hn // TILE, body, 0)
        put_partial(pt, p, nn(load_pair(tok, p), wkv[...]), pl.ds(hn, 128))

    def project_grad(p):
        def body(n, carry):
            cols = pl.ds(pl.multiple_of(n * TILE, TILE), TILE)
            put_partial(pg, p, nt(load_pair(grd, p), wo[cols, :]), cols)
            return carry

        lax.fori_loop(0, hn // TILE, body, 0)

    def rs_core(name, part, held, s0, n):
        cp.start(
            (name, "c", s0), part.at[1 - core, pl.ds(s0, n)], held.at[pl.ds(s0, n)], at_core
        )

    def rs_y1(name, part, held, r1, s0, n):
        cp.arrived((name, "c", s0))
        for s in range(s0, s0 + n):
            held[s] = held[s] + part[core, s]
        for i, d in enumerate((1, -1)):
            cp.start(
                (name, "y1", s0, d),
                held.at[pl.ds(s0, n), ring(y, 2), 8 * i : 8 * i + 8],
                r1.at[i, pl.ds(s0, n)],
                at_y(d),
            )

    def rs_y2(name, held, r1, r2, s0, n):
        cp.arrived((name, "y1", s0, 1), (name, "y1", s0, -1))
        for i, d in enumerate((1, -1)):
            t = ring(y, d)
            lo = 8 * i
            for s in range(s0, s0 + n):
                held[s, t, lo : lo + 8] = held[s, t, lo : lo + 8] + r1[i, s]
            cp.start(
                (name, "y2", s0, d), held.at[pl.ds(s0, n), t], r2.at[i, pl.ds(s0, n)], at_y(d)
            )

    def rs_wait(name, s0):
        cp.arrived((name, "y2", s0, 1), (name, "y2", s0, -1))

    def rs_value(held, r2, s):
        return held[s, y] + r2[0, s] + r2[1, s]

    def chunk_of(slot):
        bz, bx = pairs[slot // 2]
        return bz if slot % 2 == 0 else 4 + bx

    def fin_tokens(s0, n):
        rs_wait("t", s0)
        for s in range(s0, s0 + n):
            total = rs_value(xt, r2t, s).astype(BF16)
            qr[chunk_of(s)] = total[:, :hn]
            kvp[chunk_of(s)] = total[:, hn:]

    def fin_grads(s0, n):
        rs_wait("g", s0)
        for s in range(s0, s0 + n):
            gh[chunk_of(s)] = rs_value(xg, r2g, s).astype(BF16)

    def agr1(name, buf):
        mine = buf.at[:, core, y]
        for d in (1, -1):
            cp.start((name, "a", d), mine, mine, at_y(d))
        cp.start((name, "b", 0), mine, mine, at_core)

    def agr2(name, buf):
        cp.arrived((name, "a", 1), (name, "a", -1))
        for d, lo in ((1, 0), (-1, 4)):
            part = buf.at[lo : lo + 4, core, ring(y, -d)]
            cp.start((name, "c", d), part, part, at_y(d))
        for d in (1, -1):
            part = buf.at[:, core, ring(y, -d)]
            cp.start((name, "b", d), part, part, at_core)

    def agr3(name, buf):
        cp.arrived((name, "c", 1), (name, "c", -1))
        part = buf.at[:, core, ring(y, 2)]
        cp.start((name, "b", 2), part, part, at_core)

    def agr_end(name):
        cp.arrived(*[(name, "b", k) for k in (0, 1, -1, 2)])

    def rsc_far(name, make, w1):
        def put(k, cols, v):
            stfar[k // 2, pl.ds(2 * (k % 2), 2), :, cols] = v.astype(BF16)

        make(
            [(0, pairs[3][0], 0), (0, pairs[3][0], 1), (1, pairs[3][1], 0), (1, pairs[3][1], 1)],
            put,
        )
        for h in range(2):
            _, (second, _) = axes(h)
            for i, d in enumerate((1, -1)):
                cp.start((name, "f", h, d), stfar.at[h, 2 * i : 2 * i + 2], w1.at[h, i], second(d))

    def near_list(dep):
        items = []
        for h in range(2):
            for i in range(2):
                part = i if dep else 1 - i
                items.append((h, pairs[1 + i][h], part))
        return items

    def rsc_near(name, make, w1, w2, dep):
        if dep:
            for h in range(2):
                cp.arrived((name, "f", h, 1), (name, "f", h, -1))

        def put(k, cols, v):
            h, i = k // 2, k % 2
            part = i if dep else 1 - i
            if dep:
                v = v + w1[h, i, :, :, cols].astype(F32)
            stnear[h, i, pl.ds(2 * part, 2), :, cols] = v.astype(BF16)

        make(near_list(dep), put)
        for h in range(2):
            _, (second, _) = axes(h)
            for i, d in enumerate((1, -1)):
                part = i if dep else 1 - i
                cp.start(
                    (name, "n", h, d, dep),
                    stnear.at[h, i, 2 * part : 2 * part + 2],
                    w2.at[h, i, 2 * part : 2 * part + 2],
                    second(d),
                )

    def rsc_own(make):
        def put(k, cols, v):
            own[k // 2, pl.ds(2 * (k % 2), 2), :, cols] = v

        make(
            [(0, pairs[0][0], 0), (0, pairs[0][0], 1), (1, pairs[0][1], 0), (1, pairs[0][1], 1)],
            put,
        )

    def rsc_second(name, w2, v1):
        for h in range(2):
            (first, f), _ = axes(h)
            cp.arrived(*[(name, "n", h, d, dep) for d in (1, -1) for dep in (False, True)])
            for s in range(4):
                own[h, s] = own[h, s] + w2[h, 0, s].astype(F32) + w2[h, 1, s].astype(F32)
            pfar[h] = own[h, ring(f, 2)].astype(BF16)
            for i, d in enumerate((1, -1)):
                cp.start((name, "p", h, d), pfar.at[h, 16 * i : 16 * i + 16], v1.at[h, i], first(d))

    def rsc_third(name, v1, v2):
        for h in range(2):
            (first, f), _ = axes(h)
            cp.arrived((name, "p", h, 1), (name, "p", h, -1))
            for i, d in enumerate((1, -1)):
                t = ring(f, d)
                lo = 16 * i
                pnear[h, i, 16 - lo : 32 - lo] = own[h, t, 16 - lo : 32 - lo].astype(BF16)
                pnear[h, i, lo : lo + 16] = (
                    own[h, t, lo : lo + 16] + v1[h, i].astype(F32)
                ).astype(BF16)
                cp.start((name, "q", h, d), pnear.at[h, i], v2.at[h, i], first(d))

    def rsc_last(name, v2, dst, slot):
        copies = []
        for h in range(2):
            (_, f), _ = axes(h)
            cp.arrived((name, "q", h, 1), (name, "q", h, -1))
            outst[slot, h] = (
                own[h, f] + v2[h, 0].astype(F32) + v2[h, 1].astype(F32)
            ).astype(BF16)
            copy = pltpu.make_async_copy(
                outst.at[slot, h], dst.at[h * half : (h + 1) * half], out_sem.at[2 * slot + h]
            )
            copy.start()
            copies.append(copy)
        return copies

    def rsc_left(name):
        cp.left(*[(name, "f", h, d) for h in range(2) for d in (1, -1)])
        cp.left(*[(name, "n", h, d, e) for h in range(2) for d in (1, -1) for e in (False, True)])
        cp.left(*[(name, "p", h, d) for h in range(2) for d in (1, -1)])
        cp.left(*[(name, "q", h, d) for h in range(2) for d in (1, -1)])

    def rows_of(buf, items):
        return jnp.concatenate(
            [buf[4 * h + b, c].reshape(64, buf.shape[-1]) for h, b, c in items], axis=0
        )

    def make_mixed(items, put):
        def body(n, carry):
            cols = pl.ds(pl.multiple_of(n * TILE, TILE), TILE)
            v = nn(rows_of(att, items), wo[:, cols]).reshape(4, 2, 32, TILE)
            for k in range(4):
                put(k, cols, v[k])
            return carry

        lax.fori_loop(0, width // TILE, body, 0)

    def make_gtokens(items, put):
        def body(n, carry):
            cols = pl.ds(pl.multiple_of(n * TILE, TILE), TILE)
            v = nt(rows_of(gq, items), wq[cols, :]) + nt(rows_of(gkv, items), wkv[cols, :])
            v = v.reshape(4, 2, 32, TILE)
            for k in range(4):
                put(k, cols, v[k])
            return carry

        lax.fori_loop(0, width // TILE, body, 0)

    def keys():
        return kv[:, :, :, :, 0:HEAD].reshape(1024, HEAD)

    def vals():
        return kv[:, :, :, :, HEAD : 2 * HEAD].reshape(1024, HEAD)

    def attend():
        mi = mcol[...]
        mj = mrow[...]
        low = lax.shift_left(lax.shift_right_logical(mi, 10), 10)
        mask[...] = ((mj >= low) & (mj <= mi)).astype(jnp.int32)

        def body(h, carry):
            cols = pl.ds(pl.multiple_of(h * HEAD, HEAD), HEAD)
            q = qr[:, :, cols].reshape(128, HEAD)
            s = nt(q, keys()) * scale
            s = jnp.where(mask[...] > 0, s, F32(-1e30))
            e = jnp.exp(s - jnp.max(s, axis=-1, keepdims=True))
            p = e / jnp.sum(e, axis=-1, keepdims=True)
            probs[h] = p
            o = nn(p.astype(BF16), vals()).astype(BF16)
            att[:, core, y, :, cols] = o.reshape(CHUNKS, 16, HEAD)
            return carry

        lax.fori_loop(0, heads, body, 0)

    def attend_back():
        dkt[...] = jnp.zeros_like(dkt)
        dvt[...] = jnp.zeros_like(dvt)

        def body(h, carry):
            cols = pl.ds(pl.multiple_of(h * HEAD, HEAD), HEAD)
            q = qr[:, :, cols].reshape(128, HEAD)
            g = gh[:, :, cols].reshape(128, HEAD)
            p = probs[h]
            dp = nt(g, vals())
            inner = jnp.sum(p * dp, axis=-1, keepdims=True)
            ds = (p * (dp - inner) * scale).astype(BF16)
            dq = nn(ds, keys()).astype(BF16)
            gq[:, core, y, :, cols] = dq.reshape(CHUNKS, 16, HEAD)
            dkt[...] += nn(q.T, ds)
            dvt[...] += nn(g.T, p.astype(BF16))
            return carry

        lax.fori_loop(0, heads, body, 0)

    def put_dkv():
        for lo, src in ((0, dkt), (HEAD, dvt)):
            for n in range(CHUNKS):
                block = src[:, n * 128 : (n + 1) * 128].T.reshape(2, 4, 16, HEAD)
                for c in range(2):
                    pd[c, n, :, :, lo : lo + HEAD] = block[c]

    def grad_w_out():
        def body(n, carry):
            rows = pl.ds(pl.multiple_of(n * TILE, TILE), TILE)
            left = att[:, :, :, :, rows].reshape(1024, TILE)

            def inner(m, c2):
                cols = pl.ds(pl.multiple_of(m * 512, 512), 512)
                wo[rows, cols] = tn(left, grd[:, :, :, :, cols].reshape(1024, 512)).astype(BF16)
                return c2

            lax.fori_loop(0, width // 512, inner, 0)
            pltpu.make_async_copy(wo.at[rows], gwo.at[rows], out_sem.at[4 + n]).start()
            return carry

        lax.fori_loop(0, hn // TILE, body, 0)

    def grad_w_in():
        def body(n, carry):
            rows = pl.ds(pl.multiple_of(n * TILE, TILE), TILE)
            left = tok[:, :, :, :, rows].reshape(1024, TILE)

            def inner(m, c2):
                cols = pl.ds(pl.multiple_of(m * 512, 512), 512)
                wq[rows, cols] = tn(left, gq[:, :, :, :, cols].reshape(1024, 512)).astype(BF16)
                return c2

            lax.fori_loop(0, hn // 512, inner, 0)
            both = tn(left, gkv[...].reshape(1024, 128)).astype(BF16)
            wk[rows, :] = both[:, :64]
            wv[rows, :] = both[:, 64:]
            pltpu.make_async_copy(wq.at[rows], gwq.at[rows], out_sem.at[12 + n]).start()
            return carry

        lax.fori_loop(0, width // TILE, body, 0)
        pltpu.make_async_copy(wk, gwk, local.at[1]).start()
        pltpu.make_async_copy(wv, gwv, local.at[2]).start()

    ag1("t", tokens, tok)
    ag1b("t", tok)
    for copy in own_copies[0]:
        copy.wait()
    ag2("t", tok)
    ag1("g", grad_out, grd)
    for copy in loads[:3]:
        copy.wait()
    wkv[...] = jnp.concatenate([wk[...], wv[...]], axis=1)
    project(0)
    rs_core("t", pt, xt, 0, 2)
    ag1b("g", grd)
    rs_y1("t", pt, xt, r1t, 0, 2)
    ag2b("t", tok)
    for copy in own_copies[1]:
        copy.wait()
    ag2("g", grd)
    project(1)
    project(2)
    rs_core("t", pt, xt, 2, 4)
    rs_y2("t", xt, r1t, r2t, 0, 2)
    rs_y1("t", pt, xt, r1t, 2, 4)
    ag_end("t")
    project(3)
    rs_core("t", pt, xt, 6, 2)
    fin_tokens(0, 2)
    rs_y2("t", xt, r1t, r2t, 2, 4)
    rs_y1("t", pt, xt, r1t, 6, 2)
    loads[3].wait()
    project_grad(0)
    rs_core("g", pg, xg, 0, 2)
    rs_y2("t", xt, r1t, r2t, 6, 2)
    fin_tokens(2, 4)
    fin_tokens(6, 2)
    cp.start(("kv",), kvp, kvo, at_partner)
    rs_y1("g", pg, xg, r1g, 0, 2)
    ag2b("g", grd)
    cp.arrived(("kv",))
    mine, other = kvp[...].reshape(128, 128), kvo[...].reshape(128, 128)
    is_low = jnp.full((128, 128), odd, jnp.int32) == 0
    low = jnp.where(is_low, mine, other)
    high = jnp.where(is_low, other, mine)
    joined = jnp.concatenate(
        [low[:, :64], high[:, :64], low[:, 64:], high[:, 64:]], axis=1
    )
    kv[:, core, y] = joined.reshape(CHUNKS, 16, 2 * HEAD)
    agr1("k", kv)
    project_grad(1)
    agr2("k", kv)
    project_grad(2)
    agr3("k", kv)
    rs_core("g", pg, xg, 2, 4)
    rs_y2("g", xg, r1g, r2g, 0, 2)
    agr_end("k")
    rs_y1("g", pg, xg, r1g, 2, 4)
    attend()
    agr1("o", att)
    fin_grads(0, 2)
    rs_y2("g", xg, r1g, r2g, 2, 4)
    ag_end("g")
    project_grad(3)
    rs_core("g", pg, xg, 6, 2)
    agr2("o", att)
    rs_y1("g", pg, xg, r1g, 6, 2)
    agr3("o", att)
    fin_grads(2, 4)
    rs_y2("g", xg, r1g, r2g, 6, 2)
    agr_end("o")
    rsc_far("m", make_mixed, f1.at[0])
    rsc_near("m", make_mixed, f1.at[0], f2.at[0], False)
    fin_grads(6, 2)
    attend_back()
    agr1("q", gq)
    put_dkv()
    rs_core("d", pd, xd, 0, 8)
    rsc_near("m", make_mixed, f1.at[0], f2.at[0], True)
    rsc_own(make_mixed)
    rs_y1("d", pd, xd, r1d, 0, 8)
    agr2("q", gq)
    rs_y2("d", xd, r1d, r2d, 0, 8)
    grad_w_out()
    rs_wait("d", 0)
    for n in range(CHUNKS):
        dsum[n] = rs_value(xd, r2d, n)
    total = dsum[...].reshape(128, 2 * HEAD)
    lower = jnp.concatenate([total[:, 0:64], total[:, 128:192]], axis=1)
    upper = jnp.concatenate([total[:, 64:128], total[:, 192:256]], axis=1)
    dout[...] = jnp.where(is_low, upper, lower).astype(BF16)
    cp.start(("pair",), dout, dback, at_partner)
    keep = jnp.where(is_low, lower, upper)
    cp.arrived(("pair",))
    gkv[:, core, y] = (keep + dback[...].astype(F32)).astype(BF16).reshape(CHUNKS, 16, 128)
    agr1("w", gkv)
    agr3("q", gq)
    agr2("w", gkv)
    rsc_second("m", f2.at[0], n1.at[0])
    agr3("w", gkv)
    rsc_third("m", n1.at[0], n2.at[0])
    agr_end("q")
    agr_end("w")
    mixed_out = rsc_last("m", n2.at[0], mixed, 0)
    rsc_left("m")
    rsc_far("x", make_gtokens, f1.at[1])
    rsc_near("x", make_gtokens, f1.at[1], f2.at[1], False)
    rsc_own(make_gtokens)
    rsc_near("x", make_gtokens, f1.at[1], f2.at[1], True)
    grad_w_in()
    rsc_second("x", f2.at[1], n1.at[1])
    rsc_third("x", n1.at[1], n2.at[1])
    tokens_out = rsc_last("x", n2.at[1], gtokens, 1)
    for copy in mixed_out + tokens_out:
        copy.wait()
    for n in range(hn // TILE):
        rows = pl.ds(n * TILE, TILE)
        pltpu.make_async_copy(wo.at[rows], gwo.at[rows], out_sem.at[4 + n]).wait()
    for n in range(width // TILE):
        rows = pl.ds(n * TILE, TILE)
        pltpu.make_async_copy(wq.at[rows], gwq.at[rows], out_sem.at[12 + n]).wait()
    pltpu.make_async_copy(wk, gwk, local.at[1]).wait()
    pltpu.make_async_copy(wv, gwv, local.at[2]).wait()
    cp.finish()


def shards(tokens, segment_ids, w_query, w_key, value_weight, w_out, grad_out):
    width = tokens.shape[1]
    hn = w_query.shape[1]
    heads = hn // HEAD
    row = lax.axis_index("row")
    place = (segment_ids * 1024 + jnp.arange(1024, dtype=jnp.int32)).reshape(4, 4, 2, 32)
    order = jnp.stack([place[:, :, 0].transpose(1, 0, 2), place[:, :, 1]])
    order = order.reshape(CHUNKS, 2, 4, 16)
    mrow = order.reshape(1, 1024)
    mcol = lax.dynamic_slice(order, (0, row % 2, row // 2, 0), (CHUNKS, 1, 1, 16)).reshape(128, 1)

    def vm(shape, dtype=BF16):
        return pltpu.VMEM(shape, dtype)

    def rs_scratch(n):
        return [
            vm((2, CHUNKS, 4, 16, n), F32),
            vm((CHUNKS, 4, 16, n), F32),
            vm((2, CHUNKS, 8, n), F32),
            vm((2, CHUNKS, 16, n), F32),
        ]

    scratch = [
        vm((2, 4, 4, 32, width)),
        vm((2, 4, 4, 32, width)),
        vm((width, hn)),
        vm((width, 64)),
        vm((width, 64)),
        vm((width, 128)),
        vm((hn, width)),
        *rs_scratch(hn + 128),
        *rs_scratch(hn),
        *rs_scratch(2 * HEAD),
        vm((CHUNKS, 16, hn)),
        vm((CHUNKS, 16, 128)),
        vm((CHUNKS, 16, 128)),
        vm((CHUNKS, 16, hn)),
        vm((CHUNKS, 2, 4, 16, 2 * HEAD)),
        vm((128, 1024), jnp.int32),
        vm((heads, 128, 1024), F32),
        vm((HEAD, 1024), F32),
        vm((HEAD, 1024), F32),
        vm((CHUNKS, 16, 2 * HEAD), F32),
        vm((128, 128)),
        vm((128, 128)),
        vm((CHUNKS, 2, 4, 16, hn)),
        vm((CHUNKS, 2, 4, 16, hn)),
        vm((CHUNKS, 2, 4, 16, 128)),
        vm((2, 4, 32, width)),
        vm((2, 2, 4, 32, width)),
        vm((2, 4, 32, width), F32),
        vm((2, 2, 2, 2, 32, width)),
        vm((2, 2, 2, 4, 32, width)),
        vm((2, 2, 2, 16, width)),
        vm((2, 2, 2, 32, width)),
        vm((2, 32, width)),
        vm((2, 2, 32, width)),
        vm((2, 2, 32, width)),
        pltpu.SemaphoreType.DMA((SEMS,)),
        pltpu.SemaphoreType.DMA((SEMS,)),
        pltpu.SemaphoreType.DMA((8,)),
        pltpu.SemaphoreType.DMA((20,)),
    ]
    anywhere = pl.BlockSpec(memory_space=pl.ANY)
    inside = pl.BlockSpec(memory_space=pltpu.VMEM)
    shape = jax.ShapeDtypeStruct
    return pl.pallas_call(
        kernel,
        out_shape=(
            shape((64, width), BF16),
            shape((64, width), BF16),
            shape((width, hn), BF16),
            shape((width, 64), BF16),
            shape((width, 64), BF16),
            shape((hn, width), BF16),
        ),
        in_specs=[anywhere] * 6 + [inside] * 2,
        out_specs=(anywhere,) * 6,
        scratch_shapes=scratch,
        compiler_params=pltpu.CompilerParams(
            collective_id=0, has_side_effects=True, vmem_limit_bytes=VMEM_LIMIT
        ),
    )(tokens, grad_out, w_query, w_key, value_weight, w_out, mrow, mcol)


def solution(mesh):
    placed = (
        P("col", "row"),
        P(),
        P("row", "col"),
        P("row", "col"),
        P("row", "col"),
        P("col", "row"),
        P("col", "row"),
    )
    return jax.shard_map(
        shards,
        mesh=mesh,
        in_specs=placed,
        out_specs=(
            P("col", "row"),
            P("col", "row"),
            P("row", "col"),
            P("row", "col"),
            P("row", "col"),
            P("col", "row"),
        ),
        check_vma=False,
    )
```

time: 495 us -> 202 us (0.41)
  waiting for transfers between devices: 353 us -> 0 us
  Pallas kernels: 0 us -> 181 us
  matrix products: 79.7 us -> 0 us
  between operations: 14 us -> 0.71 us
  blocking collectives: 12.2 us -> 0 us
  local copies, waits for them, and re-layouts: 27.4 us -> 19.5 us
    reduce_scatter x5 -> x0, waiting for transfers between devices: 223 us -> none  [the longest x2 126 us: reduce_cols(): lax.psum_scatter(term_fn(jnp.int32(0), lax.axis_size('col') * rows_here)....]
    pallas_call x0 -> x1, Pallas kernels: none -> 181 us  [shards(): pl.pallas_call(kernel, out_shape=(shape((64, width), BF16), shape((64, wi...]
    all_gather x4 -> x0, waiting for transfers between devices: 128 us -> none  [the longest x2 88.8 us: gather_cols(): return lax.all_gather(panel, 'col', axis=0, tiled=True)]
    dot_general x11 -> x0, matrix products: 76.2 us -> none  [the longest x2 19.6 us: contract_last(): lax.dot_general(left, right, (((1,), (1,)), ((), ())), preferred_element_...]
    all_gather x1 -> x0, blocking collectives: 12.2 us -> none  [gather_rows(): return lax.all_gather(panel, 'row', axis=0, tiled=True)]
    concatenate x1 -> x0, local copies, waits for them, and re-layouts: 7.88 us -> none  [shards(): weights_in = jnp.concatenate([w_query, w_key, value_weight], axis=1)]
    slice x4 -> x1, local copies, waits for them, and re-layouts: 6.12 us -> 0.01 us  [shards(): order = jnp.stack([place[:, :, 0].transpose(1, 0, 2), place[:, :, 1]])]
    unnamed x15 -> x9, local copies, waits for them, and re-layouts: 13.2 us -> 14.1 us
  transfers between devices with their start and end apart: 11 -> 0, of which waited for: 9 -> 0; matrix products, arithmetic and copies ran while one was open for 18% -> 0% of each run, Pallas kernels for 0% -> 0%
where the time goes in v1:
time: 202 us
  Pallas kernels  181 us (90%)
  local copies, waits for them, and re-layouts  19.5 us (10%)
    pallas_call x1, Pallas kernels, shards(): pl.pallas_call(kernel, out_shape=(shape((64, width), BF16), shape((64, wi...  181 us
    unnamed x9, local copies, waits for them, and re-layouts  14.1 us

profile of v1, /device:TPU:0, one launch (start us, length us, event | category | flops | bytes accessed | tf_op | source)
XLA Modules:
  0.0 201.6 jit_solution(3687422857230242052)
XLA Ops:
  0.7 0.7 iota_add_fusion
  1.4 0.1 reshape.21
  1.5 0.7 reshape_reshape.3.mrow
  2.2 0.1 reshape.22
  2.3 0.7 reshape.24.mcol
  3.0 2.0 copy.20.wk_in
  5.0 2.0 copy.21.wv_in
  6.9 180.6 %shard_map.118 = (bf16[64,2048]{1,0:T(8,128)(2,1)}, bf16[64,2048]{1,0:T(8,128)(2,1)}, bf16[2048,1024]{1,0:T(8,128)(2,1)}, bf16[2048,64]{1,0:T(8,128)(2,1)}, bf16...) custom-call(bf16[64,2048]{1,0:T(8,128)(2,1)} %tokens.1, bf16[64,2048]{1,0:T(8,128)(2,1)} %grad_out.1, ...), custom_call_target="tpu_custom_call" | custom-call | tf_op jit(solution)/shard_map/pallas_call | solution.py:673
  187.6 1.9 copy.23
  189.5 1.9 copy.24
  191.4 1.7 copy.32
  193.1 1.7 copy.33
  194.8 0.0 copy-start
  194.8 4.8 %copy.34 = bf16[2048,1024]{1,0:T(8,128)(2,1)} copy(bf16[2048,1024]{1,0:T(8,128)(2,1)} %get-tuple-element.28) | data formatting | bytes 8388608
  199.6 0.0 copy-done
  199.6 2.0 copy.35
  (4 shorter events, 0.0 us)
Async XLA Ops:
  194.8 4.8 %copy-start = (bf16[1024,2048]{1,0:T(8,128)(2,1)S(1)}, bf16[1024,2048]{1,0:T(8,128)(2,1)}, u32[]{:S(2)}) copy-start(bf16[1024,2048]{1,0:T(8,128)(2,1)} %get-tuple-element.31) | copy-start | bytes 12582916

commit v2 on v1

v2 whole, which is shorter than its diff:
```python
import jax
import jax.numpy as jnp
from jax import lax
from jax.experimental import pallas as pl
from jax.experimental.pallas import tpu as pltpu
from jax.sharding import PartitionSpec as P

HEAD = 128
CHUNKS = 8
TILE = 256
MESH = pl.DeviceIdType.MESH
F32 = jnp.float32
BF16 = jnp.bfloat16


def nn(left, right):
    return jnp.dot(left, right, preferred_element_type=F32)


def nt(left, right):
    return lax.dot_general(left, right, (((1,), (1,)), ((), ())), preferred_element_type=F32)


def tn(left, right):
    return lax.dot_general(left, right, (((0,), (0,)), ((), ())), preferred_element_type=F32)


def ring(value, step):
    return lax.rem(value + (step + 4), 4)


class Copies:
    def __init__(self, send, recv):
        self.send, self.recv = send, recv
        self.made = {}
        self.sent = set()
        self.here = set()

    def start(self, key, src, dst, device):
        index = len(self.made)
        copy = pltpu.make_async_remote_copy(
            src_ref=src,
            dst_ref=dst,
            send_sem=self.send.at[index],
            recv_sem=self.recv.at[index],
            device_id=device,
            device_id_type=MESH,
        )
        copy.start()
        self.made[key] = copy

    def arrived(self, *keys):
        for key in keys:
            if key not in self.here:
                self.made[key].wait_recv()
                self.here.add(key)

    def left(self, *keys):
        for key in keys:
            if key not in self.sent:
                self.made[key].wait_send()
                self.sent.add(key)

    def finish(self):
        self.arrived(*list(self.made))
        self.left(*list(self.made))


SEMS = 200
STOP = None
VMEM_LIMIT = 64 * 2**20


def kernel(
    tokens, grad_out, wq_in, wk_in, wv_in, wo_in, segments,
    mixed, gtokens, gwq, gwk, gwv, gwo,
    tok, grd, wq, wkv, wo,
    pt, xt, r1t, r2t, pg, xg, lowg, r1g, r2g, pd, xd, r1d, r2d,
    qr, kvp, kvo, gh, kv, mask, probs, dkt, dvt, dsum, dout, dback, dkeep,
    att, gq, gkv,
    stfar, stnear, own, f1, f2, n1, n2, pfar, pnear, outst,
    send, recv, local, out_sem,
):
    row, col = lax.axis_index("row"), lax.axis_index("col")
    y, core = row // 2, lax.rem(row, 2)
    x, z = col // 4, lax.rem(col, 4)
    width = tok.shape[-1]
    heads = qr.shape[-1] // HEAD
    hn = heads * HEAD
    scale = HEAD ** (-0.5)

    def at_x(step):
        return {"col": ring(x, step) * 4 + z}

    def at_z(step):
        return {"col": x * 4 + ring(z, step)}

    def at_y(step):
        return {"row": ring(y, step) * 2 + core}

    at_core = {"row": y * 2 + (1 - core)}
    odd = lax.rem(z, 2)
    at_partner = {"col": x * 4 + (z + 1 - 2 * odd)}

    loads = []

    def load(src, dst):
        loads.append(pltpu.make_async_copy(src, dst, local.at[len(loads)]))

    for n in range(4):
        part = slice(n * width // 4, (n + 1) * width // 4)
        load(wq_in.at[part], wq.at[part])
    load(wk_in, wkv.at[0:64])
    load(wv_in, wkv.at[64:128])
    for n in range(4):
        part = slice(n * hn // 4, (n + 1) * hn // 4)
        load(wo_in.at[part], wo.at[part])
    leaving = []
    half = 32
    own_copies = []
    for n, (src, buf) in enumerate(((tokens, tok), (grad_out, grd))):
        own_copies.append(
            [
                pltpu.make_async_copy(src.at[0:half], buf.at[0, z, x], local.at[10 + 2 * n]),
                pltpu.make_async_copy(src.at[half:], buf.at[1, x, z], local.at[11 + 2 * n]),
            ]
        )
    for pair in own_copies:
        for copy in pair:
            copy.start()
            leaving.append(copy)
    for copy in loads:
        copy.start()
        leaving.append(copy)

    barrier = pltpu.get_barrier_semaphore()
    row_peers = [at_core] + [
        {"row": ring(y, d) * 2 + c} for d in (1, -1, 2) for c in (core, 1 - core)
    ]
    peers = [at_x(1), at_x(-1), at_z(1), at_z(-1)] + row_peers
    for device in peers:
        pl.semaphore_signal(barrier, inc=1, device_id=device, device_id_type=MESH)
    pl.semaphore_wait(barrier, len(peers))

    cp = Copies(send, recv)

    def axes(h):
        return ((at_x, x), (at_z, z)) if h == 0 else ((at_z, z), (at_x, x))

    def ag1(name, src, buf):
        for h in range(2):
            (first, f), (_, s) = axes(h)
            for d in (1, -1):
                cp.start((name, 1, h, d), src.at[h * half : (h + 1) * half], buf.at[h, s, f], first(d))

    def ag1b(name, buf):
        for h in range(2):
            (first, f), (_, s) = axes(h)
            cp.arrived((name, 1, h, 1), (name, 1, h, -1))
            for d, lo in ((1, 0), (-1, 16)):
                part = buf.at[h, s, ring(f, -d), lo : lo + 16]
                cp.start((name, 2, h, d), part, part, first(d))

    def ag2(name, buf):
        for h in range(2):
            cp.arrived((name, 2, h, 1), (name, 2, h, -1))
        for first in (True, False):
            for h in range(2):
                _, (second, s) = axes(h)
                for d in (1, -1):
                    lo = 0 if first == (d == 1) else 2
                    part = buf.at[h, s, lo : lo + 2]
                    cp.start((name, 3, h, d, first), part, part, second(d))

    def ag2b(name, buf):
        for h in range(2):
            _, (second, s) = axes(h)
            cp.arrived((name, 3, h, 1, True), (name, 3, h, -1, True))
            for d, lo in ((1, 0), (-1, 2)):
                part = buf.at[h, ring(s, -d), lo : lo + 2]
                cp.start((name, 4, h, d), part, part, second(d))

    def ag2_end(name):
        for h in range(2):
            cp.arrived((name, 3, h, 1, False), (name, 3, h, -1, False))

    def ag_end(name):
        for h in range(2):
            cp.arrived((name, 4, h, 1), (name, 4, h, -1))

    steps = ((0, 0), (-1, 1), (1, -1), (2, 2))
    pairs = [(ring(z, s), ring(x, s)) for s in (0, 1, -1, 2)]

    def load_pair(buf, p):
        parts = []
        for h, at in enumerate((z, x)):
            for c in range(2):
                part = buf[h, ring(at, steps[p][c]), 2 * c : 2 * c + 2]
                parts.append(part.reshape(64, width))
        return jnp.concatenate(parts, axis=0)

    def put_partial(dst, p, value, columns):
        size = value.shape[-1]
        five = value.reshape(2, 2, 4, 16, size)
        for h in range(2):
            for c in range(2):
                dst[c, 2 * p + h, :, :, columns] = five[h, c]

    def project(p):
        def body(n, carry):
            cols = pl.ds(pl.multiple_of(n * 512, 512), 512)
            put_partial(pt, p, nn(load_pair(tok, p), wq[:, cols]), cols)
            return carry

        lax.fori_loop(0, hn // 512, body, 0)
        put_partial(pt, p, nt(load_pair(tok, p), wkv[...]), pl.ds(hn, 128))

    def project_grad(p):
        def body(n, carry):
            cols = pl.ds(pl.multiple_of(n * 512, 512), 512)
            put_partial(pg, p, nt(load_pair(grd, p), wo[cols, :]), cols)
            return carry

        lax.fori_loop(0, hn // 512, body, 0)

    def rs_core(name, part, held, s0, n):
        cp.start(
            (name, "c", s0), part.at[1 - core, pl.ds(s0, n)], held.at[pl.ds(s0, n)], at_core
        )

    def rs_y1(name, part, held, r1, s0, n):
        cp.arrived((name, "c", s0))
        for s in range(s0, s0 + n):
            held[s] = held[s] + part[core, s]
        for i, d in enumerate((1, -1)):
            cp.start(
                (name, "y1", s0, d),
                held.at[pl.ds(s0, n), ring(y, 2), 8 * i : 8 * i + 8],
                r1.at[i, pl.ds(s0, n)],
                at_y(d),
            )

    def rs_y2(name, held, r1, r2, s0, n):
        cp.arrived((name, "y1", s0, 1), (name, "y1", s0, -1))
        for i, d in enumerate((1, -1)):
            t = ring(y, d)
            lo = 8 * i
            for s in range(s0, s0 + n):
                held[s, t, lo : lo + 8] = held[s, t, lo : lo + 8] + r1[i, s]
            cp.start(
                (name, "y2", s0, d), held.at[pl.ds(s0, n), t], r2.at[i, pl.ds(s0, n)], at_y(d)
            )

    def rs_y1_low(name, part, held, low, r1, s0, n):
        cp.arrived((name, "c", s0))
        far = ring(y, 2)
        cut = held.shape[-1] // 2
        for s in range(s0, s0 + n):
            held[s] = held[s] + part[core, s]
            low[s, far] = held[s, far].astype(BF16)
        for i, d in enumerate((1, -1)):
            cp.start(
                (name, "y1", s0, d),
                low.at[pl.ds(s0, n), far, :, i * cut : (i + 1) * cut],
                r1.at[i, pl.ds(s0, n)],
                at_y(d),
            )

    def rs_y2_low(name, held, low, r1, r2, s0, n):
        cp.arrived((name, "y1", s0, 1), (name, "y1", s0, -1))
        cut = held.shape[-1] // 2
        for i, d in enumerate((1, -1)):
            t = ring(y, d)
            mid = slice(i * cut, (i + 1) * cut)
            rest = slice((1 - i) * cut, (2 - i) * cut)
            for s in range(s0, s0 + n):
                low[s, t, :, mid] = (held[s, t, :, mid] + r1[i, s].astype(F32)).astype(BF16)
                low[s, t, :, rest] = held[s, t, :, rest].astype(BF16)
            cp.start(
                (name, "y2", s0, d), low.at[pl.ds(s0, n), t], r2.at[i, pl.ds(s0, n)], at_y(d)
            )

    def rs_wait(name, s0):
        cp.arrived((name, "y2", s0, 1), (name, "y2", s0, -1))

    def rs_value(held, r2, s):
        return held[s, y] + r2[0, s].astype(F32) + r2[1, s].astype(F32)

    def chunk_of(slot):
        low, high = steps[slot // 2]
        step = low + (high - low) * core
        return ring(z, step) if slot % 2 == 0 else 4 + ring(x, step)

    def fin_tokens(s0, n):
        rs_wait("t", s0)
        for s in range(s0, s0 + n):
            total = rs_value(xt, r2t, s).astype(BF16)
            qr[chunk_of(s)] = total[:, :hn]
            kvp[chunk_of(s)] = total[:, hn:]

    def fin_grads(s0, n):
        rs_wait("g", s0)
        for s in range(s0, s0 + n):
            gh[chunk_of(s)] = rs_value(xg, r2g, s).astype(BF16)

    def cut_of(buf, part):
        if part is None:
            return slice(None)
        size = buf.shape[-1] // 2
        return pl.ds(part * size, size)

    def agr1(name, buf, part):
        mine = buf.at[:, core, y, :, cut_of(buf, part)]
        for d in (1, -1):
            cp.start((name, "a", d), mine, mine, at_y(d))
        cp.start((name, "b", 0), mine, mine, at_core)

    def agr2(name, buf, part):
        cut = cut_of(buf, part)
        cp.arrived((name, "a", 1), (name, "a", -1))
        for d, lo in ((1, 0), (-1, 4)):
            block = buf.at[lo : lo + 4, core, ring(y, -d), :, cut]
            cp.start((name, "c", d), block, block, at_y(d))
        for d in (1, -1):
            block = buf.at[:, core, ring(y, -d), :, cut]
            cp.start((name, "b", d), block, block, at_core)

    def agr3(name, buf, part):
        cp.arrived((name, "c", 1), (name, "c", -1))
        block = buf.at[:, core, ring(y, 2), :, cut_of(buf, part)]
        cp.start((name, "b", 2), block, block, at_core)

    def agr_end(name):
        cp.arrived(*[(name, "b", k) for k in (0, 1, -1, 2)])

    def spread(name, buf):
        mine = buf.at[:, core, y]
        for n, device in enumerate(row_peers):
            cp.start((name, n), mine, mine, device)

    def spread_end(name):
        cp.arrived(*[(name, n) for n in range(len(row_peers))])

    def reuse(name, keys_):
        if name == "x":
            cp.left(*[("m", *key) for key in keys_])

    def rsc_far(name, make, w1):
        def put(k, cols, v):
            stfar[k // 2, pl.ds(2 * (k % 2), 2), :, cols] = v.astype(BF16)

        reuse(name, [("f", h, d) for h in range(2) for d in (1, -1)])
        make(
            [(0, pairs[3][0], 0), (0, pairs[3][0], 1), (1, pairs[3][1], 0), (1, pairs[3][1], 1)],
            put,
        )
        for h in range(2):
            _, (second, _) = axes(h)
            for i, d in enumerate((1, -1)):
                cp.start((name, "f", h, d), stfar.at[h, 2 * i : 2 * i + 2], w1.at[h, i], second(d))

    def near_list(dep):
        items = []
        for h in range(2):
            for i in range(2):
                part = i if dep else 1 - i
                items.append((h, pairs[1 + i][h], part))
        return items

    def rsc_near(name, make, w1, w2, dep):
        if dep:
            for h in range(2):
                cp.arrived((name, "f", h, 1), (name, "f", h, -1))

        def put(k, cols, v):
            h, i = k // 2, k % 2
            part = i if dep else 1 - i
            if dep:
                v = v + w1[h, i, :, :, cols].astype(F32)
            stnear[h, i, pl.ds(2 * part, 2), :, cols] = v.astype(BF16)

        reuse(name, [("n", h, d, e) for h in range(2) for d in (1, -1) for e in (False, True)])
        make(near_list(dep), put)
        for h in range(2):
            _, (second, _) = axes(h)
            for i, d in enumerate((1, -1)):
                part = i if dep else 1 - i
                cp.start(
                    (name, "n", h, d, dep),
                    stnear.at[h, i, 2 * part : 2 * part + 2],
                    w2.at[h, i, 2 * part : 2 * part + 2],
                    second(d),
                )

    def rsc_own(make):
        def put(k, cols, v):
            own[k // 2, pl.ds(2 * (k % 2), 2), :, cols] = v

        make(
            [(0, pairs[0][0], 0), (0, pairs[0][0], 1), (1, pairs[0][1], 0), (1, pairs[0][1], 1)],
            put,
        )

    def rsc_second(name, w2, v1):
        for h in range(2):
            (first, f), _ = axes(h)
            cp.arrived(*[(name, "n", h, d, dep) for d in (1, -1) for dep in (False, True)])
            for s in range(4):
                own[h, s] = own[h, s] + w2[h, 0, s].astype(F32) + w2[h, 1, s].astype(F32)
            reuse(name, [("p", h, 1), ("p", h, -1)])
            pfar[h] = own[h, ring(f, 2)].astype(BF16)
            for i, d in enumerate((1, -1)):
                cp.start((name, "p", h, d), pfar.at[h, 16 * i : 16 * i + 16], v1.at[h, i], first(d))

    def rsc_third(name, v1, v2):
        for h in range(2):
            (first, f), _ = axes(h)
            cp.arrived((name, "p", h, 1), (name, "p", h, -1))
            reuse(name, [("q", h, 1), ("q", h, -1)])
            for i, d in enumerate((1, -1)):
                t = ring(f, d)
                lo = 16 * i
                pnear[h, i, 16 - lo : 32 - lo] = own[h, t, 16 - lo : 32 - lo].astype(BF16)
                pnear[h, i, lo : lo + 16] = (
                    own[h, t, lo : lo + 16] + v1[h, i].astype(F32)
                ).astype(BF16)
                cp.start((name, "q", h, d), pnear.at[h, i], v2.at[h, i], first(d))

    def rsc_last(name, v2, dst, slot):
        for h in range(2):
            (_, f), _ = axes(h)
            cp.arrived((name, "q", h, 1), (name, "q", h, -1))
            outst[slot, h] = (
                own[h, f] + v2[h, 0].astype(F32) + v2[h, 1].astype(F32)
            ).astype(BF16)
            copy = pltpu.make_async_copy(
                outst.at[slot, h], dst.at[h * half : (h + 1) * half], out_sem.at[2 * slot + h]
            )
            copy.start()
            leaving.append(copy)

    def rows_of(buf, items):
        return jnp.concatenate(
            [buf[4 * h + b, c].reshape(64, buf.shape[-1]) for h, b, c in items], axis=0
        )

    def make_mixed(items, put):
        def body(n, carry):
            cols = pl.ds(pl.multiple_of(n * 1024, 1024), 1024)
            v = nn(rows_of(att, items), wo[:, cols]).reshape(4, 2, 32, 1024)
            for k in range(4):
                put(k, cols, v[k])
            return carry

        lax.fori_loop(0, width // 1024, body, 0)

    def make_gtokens(items, put):
        def body(n, carry):
            cols = pl.ds(pl.multiple_of(n * 1024, 1024), 1024)
            v = nt(rows_of(gq, items), wq[cols, :]) + nn(rows_of(gkv, items), wkv[:, cols])
            v = v.reshape(4, 2, 32, 1024)
            for k in range(4):
                put(k, cols, v[k])
            return carry

        lax.fori_loop(0, width // 1024, body, 0)

    def keys():
        return kv[:, :, :, :, 0:HEAD].reshape(1024, HEAD)

    def vals():
        return kv[:, :, :, :, HEAD : 2 * HEAD].reshape(1024, HEAD)

    def place(p):
        i, s, b, h = p & 31, (p >> 5) & 3, (p >> 7) & 3, p >> 9
        xs = jnp.where(h == 0, s, b)
        zs = jnp.where(h == 0, b, s)
        return xs * 256 + zs * 64 + h * 32 + i

    def make_mask():
        seg = segments[...].astype(F32)
        seg = jnp.concatenate([seg[n : n + 1] for n in range(8)], axis=1)
        shape = (1024, 1024)
        key_place = place(lax.broadcasted_iota(jnp.int32, (1, 1024), 1))
        pick = lax.broadcasted_iota(jnp.int32, shape, 0) == key_place
        key_seg = nn(
            jnp.broadcast_to(seg, (16, 1024)).astype(BF16), pick.astype(F32).astype(BF16)
        )[0:1]
        r = lax.broadcasted_iota(jnp.int32, (128, 1), 0)
        mine = place(((r >> 4) << 7) + core * 64 + y * 16 + (r & 15))
        here = lax.broadcasted_iota(jnp.int32, (128, 1024), 1) == mine
        my_seg = jnp.sum(jnp.where(here, seg, F32(0)), axis=1, keepdims=True)
        mask[...] = ((my_seg == key_seg) & (key_place <= mine)).astype(jnp.int32)

    def attend(part):
        def body(h, carry):
            cols = pl.ds(pl.multiple_of(h * HEAD, HEAD), HEAD)
            q = qr[:, :, cols].reshape(128, HEAD)
            s = nt(q, keys()) * scale
            s = jnp.where(mask[...] > 0, s, F32(-1e30))
            e = jnp.exp(s - jnp.max(s, axis=-1, keepdims=True))
            p = e / jnp.sum(e, axis=-1, keepdims=True)
            probs[h] = p
            o = nn(p.astype(BF16), vals()).astype(BF16)
            att[:, core, y, :, cols] = o.reshape(CHUNKS, 16, HEAD)
            return carry

        lax.fori_loop(part * heads // 4, (part + 1) * heads // 4, body, 0)

    def attend_back(part):
        if part == 0:
            dkt[...] = jnp.zeros_like(dkt)
            dvt[...] = jnp.zeros_like(dvt)

        def body(h, carry):
            cols = pl.ds(pl.multiple_of(h * HEAD, HEAD), HEAD)
            q = qr[:, :, cols].reshape(128, HEAD)
            g = gh[:, :, cols].reshape(128, HEAD)
            p = probs[h]
            dp = nt(g, vals())
            inner = jnp.sum(p * dp, axis=-1, keepdims=True)
            ds = (p * (dp - inner) * scale).astype(BF16)
            probs[h] = ds.astype(F32)
            dkt[...] += nn(q.T, ds)
            dvt[...] += nn(g.T, p.astype(BF16))
            return carry

        lax.fori_loop(part * heads // 4, (part + 1) * heads // 4, body, 0)

    def grad_query(part):
        def body(h, carry):
            cols = pl.ds(pl.multiple_of(h * HEAD, HEAD), HEAD)
            dq = nn(probs[h].astype(BF16), keys()).astype(BF16)
            gq[:, core, y, :, cols] = dq.reshape(CHUNKS, 16, HEAD)
            return carry

        lax.fori_loop(part * heads // 2, (part + 1) * heads // 2, body, 0)

    def put_dkv():
        for lo, src in ((0, dkt), (HEAD, dvt)):
            for n in range(CHUNKS):
                block = src[:, n * 128 : (n + 1) * 128].T.reshape(2, 4, 16, HEAD)
                for c in range(2):
                    pd[c, n, :, :, lo : lo + HEAD] = block[c]

    def grad_w_out(part):
        size = hn // 4
        rows = slice(part * size, (part + 1) * size)

        def body(m, carry):
            cols = pl.ds(pl.multiple_of(m * 1024, 1024), 1024)
            left = att[:, :, :, :, rows].reshape(1024, size)
            wo[rows, cols] = tn(left, grd[:, :, :, :, cols].reshape(1024, 1024)).astype(BF16)
            return carry

        lax.fori_loop(0, width // 1024, body, 0)
        copy = pltpu.make_async_copy(wo.at[rows], gwo.at[rows], out_sem.at[4 + part])
        copy.start()
        leaving.append(copy)

    def grad_w_in(part):
        size = width // 4
        rows = slice(part * size, (part + 1) * size)

        def body(m, carry):
            cols = pl.ds(pl.multiple_of(m * 512, 512), 512)
            left = tok[:, :, :, :, rows].reshape(1024, size)
            wq[rows, cols] = tn(left, gq[:, :, :, :, cols].reshape(1024, 512)).astype(BF16)
            return carry

        lax.fori_loop(0, hn // 512, body, 0)
        left = tok[:, :, :, :, rows].reshape(1024, size)
        wkv[:, rows] = tn(gkv[...].reshape(1024, 128), left).astype(BF16)
        moves = [(wq.at[rows], gwq.at[rows])]
        if part == 3:
            moves += [(wkv.at[0:64], gwk), (wkv.at[64:128], gwv)]
        for n, (src, dst) in enumerate(moves):
            copy = pltpu.make_async_copy(src, dst, out_sem.at[8 + part + n])
            copy.start()
            leaving.append(copy)

    is_low = jnp.full((128, 128), odd, jnp.int32) == 0

    def wait_local(copies):
        for copy in copies:
            copy.wait()
            leaving[:] = [c for c in leaving if c is not copy]

    def join_start():
        cp.start(("kv",), kvp, kvo, at_partner)

    def join_end():
        cp.arrived(("kv",))
        mine, other = kvp[...].reshape(128, 128), kvo[...].reshape(128, 128)
        low = jnp.where(is_low, mine, other)
        high = jnp.where(is_low, other, mine)
        joined = jnp.concatenate([low[:, :64], high[:, :64], low[:, 64:], high[:, 64:]], axis=1)
        kv[:, core, y] = joined.reshape(CHUNKS, 16, 2 * HEAD)

    def split_start():
        rs_wait("d", 0)
        for n in range(CHUNKS):
            dsum[n] = rs_value(xd, r2d, n)
        total = dsum[...].reshape(128, 2 * HEAD)
        lower = jnp.concatenate([total[:, 0:64], total[:, 128:192]], axis=1)
        upper = jnp.concatenate([total[:, 64:128], total[:, 192:256]], axis=1)
        dout[...] = jnp.where(is_low, upper, lower).astype(BF16)
        cp.start(("pair",), dout, dback, at_partner)
        dkeep[...] = jnp.where(is_low, lower, upper)

    def split_end():
        cp.arrived(("pair",))
        kept = (dkeep[...] + dback[...].astype(F32)).astype(BF16)
        gkv[:, core, y] = kept.reshape(CHUNKS, 16, 128)

    work = [
        (ag1, "t", tokens, tok),
        (wait_local, own_copies[0]),
        (ag1, "g", grad_out, grd),
        (wait_local, own_copies[1]),
        (make_mask,),
        (wait_local, loads[0:6]),
        (ag1b, "t", tok),
        (wait_local, loads[6:]),
        (ag1b, "g", grd),
        (ag2, "t", tok),
        (project, 0),
        (rs_core, "t", pt, xt, 0, 2),
        (rs_y1, "t", pt, xt, r1t, 0, 2),
        (ag2b, "t", tok),
        (ag2, "g", grd),
        (rs_y2, "t", xt, r1t, r2t, 0, 2),
        (project, 1),
        (rs_core, "t", pt, xt, 2, 2),
        (project_grad, 0),
        (rs_core, "g", pg, xg, 0, 2),
        (rs_y1, "t", pt, xt, r1t, 2, 2),
        (fin_tokens, 0, 2),
        (ag2_end, "t"),
        (project, 2),
        (rs_core, "t", pt, xt, 4, 2),
        (rs_y1_low, "g", pg, xg, lowg, r1g, 0, 2),
        (rs_y2, "t", xt, r1t, r2t, 2, 2),
        (rs_y1, "t", pt, xt, r1t, 4, 2),
        (rs_y2_low, "g", xg, lowg, r1g, r2g, 0, 2),
        (ag_end, "t"),
        (project, 3),
        (rs_core, "t", pt, xt, 6, 2),
        (fin_tokens, 2, 2),
        (rs_y2, "t", xt, r1t, r2t, 4, 2),
        (rs_y1, "t", pt, xt, r1t, 6, 2),
        (fin_grads, 0, 2),
        (ag2b, "g", grd),
        (project_grad, 1),
        (rs_core, "g", pg, xg, 2, 2),
        (fin_tokens, 4, 2),
        (rs_y2, "t", xt, r1t, r2t, 6, 2),
        (rs_y1_low, "g", pg, xg, lowg, r1g, 2, 2),
        (ag2_end, "g"),
        (project_grad, 2),
        (rs_core, "g", pg, xg, 4, 2),
        (fin_tokens, 6, 2),
        (join_start,),
        (rs_y2_low, "g", xg, lowg, r1g, r2g, 2, 2),
        (rs_y1_low, "g", pg, xg, lowg, r1g, 4, 2),
        (join_end,),
        (agr1, "k", kv, None),
        (ag_end, "g"),
        (project_grad, 3),
        (rs_core, "g", pg, xg, 6, 2),
        (rs_y2_low, "g", xg, lowg, r1g, r2g, 4, 2),
        (fin_grads, 2, 2),
        (agr2, "k", kv, None),
        (rs_y1_low, "g", pg, xg, lowg, r1g, 6, 2),
        (fin_grads, 4, 2),
        (agr3, "k", kv, None),
        (rs_y2_low, "g", xg, lowg, r1g, r2g, 6, 2),
        (agr_end, "k"),
        (attend, 0),
        (attend, 1),
        (agr1, "o0", att, 0),
        (fin_grads, 6, 2),
        (attend, 2),
        (attend, 3),
        (agr1, "o1", att, 1),
        (attend_back, 0),
        (agr2, "o0", att, 0),
        (attend_back, 1),
        (attend_back, 2),
        (agr3, "o0", att, 0),
        (agr2, "o1", att, 1),
        (attend_back, 3),
        (agr_end, "o0"),
        (put_dkv,),
        (rs_core, "d", pd, xd, 0, 8),
        (agr3, "o1", att, 1),
        (grad_query, 0),
        (agr1, "q0", gq, 0),
        (grad_query, 1),
        (agr1, "q1", gq, 1),
        (rs_y1, "d", pd, xd, r1d, 0, 8),
        (agr_end, "o1"),
        (rsc_far, "m", make_mixed, f1.at[0]),
        (rsc_near, "m", make_mixed, f1.at[0], f2.at[0], False),
        (agr2, "q0", gq, 0),
        (rsc_own, make_mixed),
        (agr2, "q1", gq, 1),
        (rs_y2, "d", xd, r1d, r2d, 0, 8),
        (agr3, "q0", gq, 0),
        (rsc_near, "m", make_mixed, f1.at[0], f2.at[0], True),
        (agr_end, "q0"),
        (agr3, "q1", gq, 1),
        (grad_w_out, 0),
        (agr_end, "q1"),
        (grad_w_out, 1),
        (split_start,),
        (grad_w_out, 2),
        (grad_w_out, 3),
        (split_end,),
        (spread, "w", gkv),
        (rsc_second, "m", f2.at[0], n1.at[0]),
        (spread_end, "w"),
        (rsc_far, "x", make_gtokens, f1.at[1]),
        (rsc_third, "m", n1.at[0], n2.at[0]),
        (rsc_near, "x", make_gtokens, f1.at[1], f2.at[1], False),
        (rsc_near, "x", make_gtokens, f1.at[1], f2.at[1], True),
        (rsc_last, "m", n2.at[0], mixed, 0),
        (rsc_own, make_gtokens),
        (grad_w_in, 0),
        (grad_w_in, 1),
        (grad_w_in, 2),
        (grad_w_in, 3),
        (rsc_second, "x", f2.at[1], n1.at[1]),
        (rsc_third, "x", n1.at[1], n2.at[1]),
        (rsc_last, "x", n2.at[1], gtokens, 1),
    ]
    for step in work[:STOP]:
        step[0](*step[1:])
    wait_local(list(leaving))
    cp.finish()


def hand_over(arrays):
    count = len(arrays)
    pieces = [max(1, a.size // 2**18) for a in arrays]
    total = sum(pieces)

    def body(*refs):
        sources, results, held = refs[:count], refs[count : 2 * count], refs[2 * count : 3 * count]
        came, went = refs[-2:]
        moves = []
        for n in range(count):
            rows = arrays[n].shape[0] // pieces[n]
            for k in range(pieces[n]):
                at, m = pl.ds(k * rows, rows), len(moves)
                moves.append(
                    (
                        pltpu.make_async_copy(sources[n].at[at], held[n].at[at], came.at[m]),
                        pltpu.make_async_copy(held[n].at[at], results[n].at[at], went.at[m]),
                    )
                )
        for come, _ in moves:
            come.start()
        for come, go in moves:
            come.wait()
            go.start()
        for _, go in moves:
            go.wait()

    anywhere = pl.BlockSpec(memory_space=pl.ANY)
    return pl.pallas_call(
        body,
        out_shape=tuple(jax.ShapeDtypeStruct(a.shape, a.dtype) for a in arrays),
        in_specs=[anywhere] * count,
        out_specs=(anywhere,) * count,
        scratch_shapes=[
            *(pltpu.VMEM(a.shape, a.dtype) for a in arrays),
            pltpu.SemaphoreType.DMA((total,)),
            pltpu.SemaphoreType.DMA((total,)),
        ],
        compiler_params=pltpu.CompilerParams(vmem_limit_bytes=32 * 2**20),
    )(*arrays)


def shards(tokens, segment_ids, w_query, w_key, value_weight, w_out, grad_out):
    width = tokens.shape[1]
    hn = w_query.shape[1]
    heads = hn // HEAD
    def vm(shape, dtype=BF16):
        return pltpu.VMEM(shape, dtype)

    def rs_scratch(n):
        return [
            vm((2, CHUNKS, 4, 16, n), F32),
            vm((CHUNKS, 4, 16, n), F32),
            vm((2, CHUNKS, 8, n), F32),
            vm((2, CHUNKS, 16, n), F32),
        ]

    scratch = [
        vm((2, 4, 4, 32, width)),
        vm((2, 4, 4, 32, width)),
        vm((width, hn)),
        vm((128, width)),
        vm((hn, width)),
        *rs_scratch(hn + 128),
        vm((2, CHUNKS, 4, 16, hn), F32),
        vm((CHUNKS, 4, 16, hn), F32),
        vm((CHUNKS, 4, 16, hn)),
        vm((2, CHUNKS, 16, hn // 2)),
        vm((2, CHUNKS, 16, hn)),
        *rs_scratch(2 * HEAD),
        vm((CHUNKS, 16, hn)),
        vm((CHUNKS, 16, 128)),
        vm((CHUNKS, 16, 128)),
        vm((CHUNKS, 16, hn)),
        vm((CHUNKS, 2, 4, 16, 2 * HEAD)),
        vm((128, 1024), jnp.int32),
        vm((heads, 128, 1024), F32),
        vm((HEAD, 1024), F32),
        vm((HEAD, 1024), F32),
        vm((CHUNKS, 16, 2 * HEAD), F32),
        vm((128, 128)),
        vm((128, 128)),
        vm((128, 128), F32),
        vm((CHUNKS, 2, 4, 16, hn)),
        vm((CHUNKS, 2, 4, 16, hn)),
        vm((CHUNKS, 2, 4, 16, 128)),
        vm((2, 4, 32, width)),
        vm((2, 2, 4, 32, width)),
        vm((2, 4, 32, width), F32),
        vm((2, 2, 2, 2, 32, width)),
        vm((2, 2, 2, 4, 32, width)),
        vm((2, 2, 2, 16, width)),
        vm((2, 2, 2, 32, width)),
        vm((2, 32, width)),
        vm((2, 2, 32, width)),
        vm((2, 2, 32, width)),
        pltpu.SemaphoreType.DMA((SEMS,)),
        pltpu.SemaphoreType.DMA((SEMS,)),
        pltpu.SemaphoreType.DMA((16,)),
        pltpu.SemaphoreType.DMA((20,)),
    ]
    anywhere = pl.BlockSpec(memory_space=pl.ANY)
    inside = pl.BlockSpec(memory_space=pltpu.VMEM)
    shape = jax.ShapeDtypeStruct
    made = pl.pallas_call(
        kernel,
        out_shape=(
            shape((64, width), BF16),
            shape((64, width), BF16),
            shape((width, hn), BF16),
            shape((64, width), BF16),
            shape((64, width), BF16),
            shape((hn, width), BF16),
        ),
        in_specs=[anywhere] * 6 + [inside],
        out_specs=(anywhere,) * 6,
        scratch_shapes=scratch,
        compiler_params=pltpu.CompilerParams(
            collective_id=0, has_side_effects=True, vmem_limit_bytes=VMEM_LIMIT
        ),
    )(
        tokens, grad_out, w_query, w_key.T, value_weight.T, w_out, segment_ids.reshape(8, 128)
    )
    mixed, gtokens, gwq, gwk, gwv, gwo = hand_over(made)
    return mixed, gtokens, gwq, gwk.T, gwv.T, gwo


def solution(mesh):
    placed = (
        P("col", "row"),
        P(),
        P("row", "col"),
        P("row", "col"),
        P("row", "col"),
        P("col", "row"),
        P("col", "row"),
    )
    return jax.shard_map(
        shards,
        mesh=mesh,
        in_specs=placed,
        out_specs=(
            P("col", "row"),
            P("col", "row"),
            P("row", "col"),
            P("row", "col"),
            P("row", "col"),
            P("col", "row"),
        ),
        check_vma=False,
    )
```

time: 202 us -> 159 us (0.79)
  Pallas kernels: 181 us -> 150 us
  local copies, waits for them, and re-layouts: 19.5 us -> 8.17 us
    pallas_call x1, Pallas kernels: 181 us -> 145 us  [shards(): pl.pallas_call(kernel, out_shape=(shape((64, width), BF16), shape((64, wi...]
    unnamed x9 -> x12, local copies, waits for them, and re-layouts: 14.1 us -> 8.17 us
    pallas_call x0 -> x1, Pallas kernels: none -> 4.58 us  [hand_over(): pl.pallas_call(body, out_shape=tuple((jax.ShapeDtypeStruct(a.shape, a.dty...]
    pallas_call x2 -> x0, local copies, waits for them, and re-layouts: 3.87 us -> none  [shards(): pl.pallas_call(kernel, out_shape=(shape((64, width), BF16), shape((64, wi...]
where the time goes in v2:
time: 159 us
  Pallas kernels  150 us (94%)
  local copies, waits for them, and re-layouts  8.17 us (5%)
    pallas_call x1, Pallas kernels, shards(): pl.pallas_call(kernel, out_shape=(shape((64, width), BF16), shape((64, wi...  145 us
    unnamed x12, local copies, waits for them, and re-layouts  8.17 us
    pallas_call x1, Pallas kernels, hand_over(): pl.pallas_call(body, out_shape=tuple((jax.ShapeDtypeStruct(a.shape, a.dty...  4.58 us

profile of v2, /device:TPU:0, one launch (start us, length us, event | category | flops | bytes accessed | tf_op | source)
XLA Modules:
  0.0 158.9 jit_solution(13309314528787876446)
XLA Ops:
  0.6 145.3 %shard_map.118 = (bf16[64,2048]{1,0:T(8,128)(2,1)}, bf16[64,2048]{1,0:T(8,128)(2,1)}, bf16[2048,1024]{1,0:T(8,128)(2,1)}, bf16[64,2048]{1,0:T(8,128)(2,1)}, bf16...) custom-call(bf16[64,2048]{1,0:T(8,128)(2,1)} %tokens.1, bf16[64,2048]{1,0:T(8,128)(2,1)} %grad_out.1, ...), custom_call_target="tpu_custom_call" | custom-call | tf_op jit(solution)/shard_map/pallas_call | solution.py:847
  145.9 0.0 copy-start
  146.0 2.2 %copy-done = bf16[2048,1024]{1,0:T(8,128)(2,1)S(1)} copy-done((bf16[2048,1024]{1,0:T(8,128)(2,1)S(1)}, bf16[2048,1024]{1,0:T(8,128)(2,1)}, u32[]{:S(2)}) %copy-start) | copy-done | bytes 4194328
  148.1 0.0 copy-start.1
  148.1 2.2 %copy-done.1 = bf16[1024,2048]{1,0:T(8,128)(2,1)S(1)} copy-done((bf16[1024,2048]{1,0:T(8,128)(2,1)S(1)}, bf16[1024,2048]{1,0:T(8,128)(2,1)}, u32[]{:S(2)}) %copy-start.1) | copy-done | bytes 4194328
  150.3 0.0 copy-start.2
  150.3 0.9 copy-done.2
  151.3 0.0 copy-start.3
  151.3 0.9 copy-done.3
  152.2 0.0 copy-start.4
  152.2 0.9 copy-done.4
  153.2 0.0 copy-start.5
  153.2 0.9 copy-done.5
  154.1 4.6 %shard_map.119 = (bf16[64,2048]{1,0:T(8,128)(2,1)}, bf16[64,2048]{1,0:T(8,128)(2,1)}, bf16[2048,1024]{1,0:T(8,128)(2,1)}, bf16[64,2048]{1,0:T(8,128)(2,1)}, bf16...) custom-call(bf16[64,2048]{1,0:T(8,128)(2,1)S(1)} %copy-done.2, bf16[64,2048]{1,0:T(8,128)(2,1)S(1)} %copy-done.3, ...), custom_call_target="tpu_custom_call" | custom-call | tf_op jit(solution)/shard_map/pallas_call | solution.py:771
Async XLA Ops:
  145.9 2.2 %copy-start = (bf16[2048,1024]{1,0:T(8,128)(2,1)S(1)}, bf16[2048,1024]{1,0:T(8,128)(2,1)}, u32[]{:S(2)}) copy-start(bf16[2048,1024]{1,0:T(8,128)(2,1)} %get-tuple-element.20.refs_2_) | copy-start | bytes 12582916
  148.1 2.2 %copy-start.1 = (bf16[1024,2048]{1,0:T(8,128)(2,1)S(1)}, bf16[1024,2048]{1,0:T(8,128)(2,1)}, u32[]{:S(2)}) copy-start(bf16[1024,2048]{1,0:T(8,128)(2,1)} %get-tuple-element.23.refs_5_) | copy-start | bytes 12582916
  150.3 0.9 copy-start.2
  151.3 0.9 copy-start.3
  152.2 0.9 copy-start.4
  153.2 0.9 copy-start.5

commit v3 on v2

--- a/solution.py
+++ b/solution.py
@@ -66,7 +66,7 @@
         self.left(*list(self.made))
 
 
-SEMS = 200
+SEMS = 240
 STOP = None
 VMEM_LIMIT = 64 * 2**20
 
@@ -75,7 +75,7 @@
     tokens, grad_out, wq_in, wk_in, wv_in, wo_in, segments,
     mixed, gtokens, gwq, gwk, gwv, gwo,
     tok, grd, wq, wkv, wo,
-    pt, xt, r1t, r2t, pg, xg, lowg, r1g, r2g, pd, xd, r1d, r2d,
+    pt, xt, r1t, r2t, pv, xv, r1v, r2v, pg, xg, lowg, r1g, r2g, pd, xd, r1d, r2d,
     qr, kvp, kvo, gh, kv, mask, probs, dkt, dvt, dsum, dout, dback, dkeep,
     att, gq, gkv,
     stfar, stnear, own, f1, f2, n1, n2, pfar, pnear, outst,
@@ -213,7 +213,9 @@
             return carry
 
         lax.fori_loop(0, hn // 512, body, 0)
-        put_partial(pt, p, nt(load_pair(tok, p), wkv[...]), pl.ds(hn, 128))
+
+    def project_kv(p):
+        put_partial(pv, p, nt(load_pair(tok, p), wkv[...]), pl.ds(0, 128))
 
     def project_grad(p):
         def body(n, carry):
@@ -294,9 +296,12 @@
     def fin_tokens(s0, n):
         rs_wait("t", s0)
         for s in range(s0, s0 + n):
-            total = rs_value(xt, r2t, s).astype(BF16)
-            qr[chunk_of(s)] = total[:, :hn]
-            kvp[chunk_of(s)] = total[:, hn:]
+            qr[chunk_of(s)] = rs_value(xt, r2t, s).astype(BF16)
+
+    def fin_kv(s0, n):
+        rs_wait("v", s0)
+        for s in range(s0, s0 + n):
+            kvp[chunk_of(s)] = rs_value(xv, r2v, s).astype(BF16)
 
     def fin_grads(s0, n):
         rs_wait("g", s0)
@@ -345,96 +350,117 @@
         if name == "x":
             cp.left(*[("m", *key) for key in keys_])
 
-    def rsc_far(name, make, w1):
-        def put(k, cols, v):
-            stfar[k // 2, pl.ds(2 * (k % 2), 2), :, cols] = v.astype(BF16)
-
-        reuse(name, [("f", h, d) for h in range(2) for d in (1, -1)])
-        make(
+    cw = width // 2
+
+    def rsc_far(name, make, w1, part):
+        cols = slice(part * cw, (part + 1) * cw)
+        reuse(name, [("f", h, d, part) for h in range(2) for d in (1, -1)])
+        v = make(
             [(0, pairs[3][0], 0), (0, pairs[3][0], 1), (1, pairs[3][1], 0), (1, pairs[3][1], 1)],
-            put,
+            cols,
         )
         for h in range(2):
             _, (second, _) = axes(h)
             for i, d in enumerate((1, -1)):
-                cp.start((name, "f", h, d), stfar.at[h, 2 * i : 2 * i + 2], w1.at[h, i], second(d))
-
-    def near_list(dep):
-        items = []
-        for h in range(2):
-            for i in range(2):
-                part = i if dep else 1 - i
-                items.append((h, pairs[1 + i][h], part))
-        return items
-
-    def rsc_near(name, make, w1, w2, dep):
-        if dep:
-            for h in range(2):
-                cp.arrived((name, "f", h, 1), (name, "f", h, -1))
-
-        def put(k, cols, v):
-            h, i = k // 2, k % 2
-            part = i if dep else 1 - i
-            if dep:
-                v = v + w1[h, i, :, :, cols].astype(F32)
-            stnear[h, i, pl.ds(2 * part, 2), :, cols] = v.astype(BF16)
-
-        reuse(name, [("n", h, d, e) for h in range(2) for d in (1, -1) for e in (False, True)])
-        make(near_list(dep), put)
-        for h in range(2):
-            _, (second, _) = axes(h)
-            for i, d in enumerate((1, -1)):
-                part = i if dep else 1 - i
+                stfar[h, 2 * i : 2 * i + 2, :, cols] = v[2 * h + i].astype(BF16)
                 cp.start(
-                    (name, "n", h, d, dep),
-                    stnear.at[h, i, 2 * part : 2 * part + 2],
-                    w2.at[h, i, 2 * part : 2 * part + 2],
+                    (name, "f", h, d, part),
+                    stfar.at[h, 2 * i : 2 * i + 2, :, cols],
+                    w1.at[h, i, :, :, cols],
                     second(d),
                 )
 
-    def rsc_own(make):
-        def put(k, cols, v):
-            own[k // 2, pl.ds(2 * (k % 2), 2), :, cols] = v
-
-        make(
+    def rsc_near(name, make, w1, w2, dep, part):
+        cols = slice(part * cw, (part + 1) * cw)
+        items = []
+        for h in range(2):
+            for i in range(2):
+                items.append((h, pairs[1 + i][h], i if dep else 1 - i))
+        v = make(items, cols)
+        for h in range(2):
+            _, (second, _) = axes(h)
+            if dep:
+                cp.arrived((name, "f", h, 1, part), (name, "f", h, -1, part))
+            for i, d in enumerate((1, -1)):
+                reuse(name, [("n", h, d, dep, part)])
+                at = 2 * i if dep else 2 - 2 * i
+                value = v[2 * h + i]
+                if dep:
+                    value = value + w1[h, i, :, :, cols].astype(F32)
+                stnear[h, i, at : at + 2, :, cols] = value.astype(BF16)
+                cp.start(
+                    (name, "n", h, d, dep, part),
+                    stnear.at[h, i, at : at + 2, :, cols],
+                    w2.at[h, i, at : at + 2, :, cols],
+                    second(d),
+                )
+
+    def rsc_own(make, part):
+        cols = slice(part * cw, (part + 1) * cw)
+        v = make(
             [(0, pairs[0][0], 0), (0, pairs[0][0], 1), (1, pairs[0][1], 0), (1, pairs[0][1], 1)],
-            put,
+            cols,
         )
-
-    def rsc_second(name, w2, v1):
+        for h in range(2):
+            for i in range(2):
+                own[h, 2 * i : 2 * i + 2, :, cols] = v[2 * h + i]
+
+    def rsc_second(name, w2, v1, part):
+        cols = slice(part * cw, (part + 1) * cw)
         for h in range(2):
             (first, f), _ = axes(h)
-            cp.arrived(*[(name, "n", h, d, dep) for d in (1, -1) for dep in (False, True)])
-            for s in range(4):
-                own[h, s] = own[h, s] + w2[h, 0, s].astype(F32) + w2[h, 1, s].astype(F32)
-            reuse(name, [("p", h, 1), ("p", h, -1)])
-            pfar[h] = own[h, ring(f, 2)].astype(BF16)
-            for i, d in enumerate((1, -1)):
-                cp.start((name, "p", h, d), pfar.at[h, 16 * i : 16 * i + 16], v1.at[h, i], first(d))
-
-    def rsc_third(name, v1, v2):
+            cp.arrived(*[(name, "n", h, d, dep, part) for d in (1, -1) for dep in (False, True)])
+            for k in (2, 1, -1, 0):
+                s = ring(f, k)
+                own[h, s, :, cols] = (
+                    own[h, s, :, cols]
+                    + w2[h, 0, s, :, cols].astype(F32)
+                    + w2[h, 1, s, :, cols].astype(F32)
+                )
+                if k == 2:
+                    reuse(name, [("p", h, 1, part), ("p", h, -1, part)])
+                    pfar[h, :, cols] = own[h, s, :, cols].astype(BF16)
+                    for i, d in enumerate((1, -1)):
+                        lo = 16 * i
+                        cp.start(
+                            (name, "p", h, d, part),
+                            pfar.at[h, lo : lo + 16, cols],
+                            v1.at[h, i, :, cols],
+                            first(d),
+                        )
+
+    def rsc_third(name, v1, v2, part):
+        cols = slice(part * cw, (part + 1) * cw)
         for h in range(2):
             (first, f), _ = axes(h)
-            cp.arrived((name, "p", h, 1), (name, "p", h, -1))
-            reuse(name, [("q", h, 1), ("q", h, -1)])
+            cp.arrived((name, "p", h, 1, part), (name, "p", h, -1, part))
+            reuse(name, [("q", h, 1, part), ("q", h, -1, part)])
             for i, d in enumerate((1, -1)):
                 t = ring(f, d)
-                lo = 16 * i
-                pnear[h, i, 16 - lo : 32 - lo] = own[h, t, 16 - lo : 32 - lo].astype(BF16)
-                pnear[h, i, lo : lo + 16] = (
-                    own[h, t, lo : lo + 16] + v1[h, i].astype(F32)
+                mid = slice(16 * i, 16 * i + 16)
+                rest = slice(16 - 16 * i, 32 - 16 * i)
+                pnear[h, i, rest, cols] = own[h, t, rest, cols].astype(BF16)
+                pnear[h, i, mid, cols] = (
+                    own[h, t, mid, cols] + v1[h, i, :, cols].astype(F32)
                 ).astype(BF16)
-                cp.start((name, "q", h, d), pnear.at[h, i], v2.at[h, i], first(d))
-
-    def rsc_last(name, v2, dst, slot):
+                cp.start(
+                    (name, "q", h, d, part), pnear.at[h, i, :, cols], v2.at[h, i, :, cols], first(d)
+                )
+
+    def rsc_last(name, v2, dst, slot, part):
+        cols = slice(part * cw, (part + 1) * cw)
         for h in range(2):
             (_, f), _ = axes(h)
-            cp.arrived((name, "q", h, 1), (name, "q", h, -1))
-            outst[slot, h] = (
-                own[h, f] + v2[h, 0].astype(F32) + v2[h, 1].astype(F32)
+            cp.arrived((name, "q", h, 1, part), (name, "q", h, -1, part))
+            outst[slot, h, :, cols] = (
+                own[h, f, :, cols]
+                + v2[h, 0, :, cols].astype(F32)
+                + v2[h, 1, :, cols].astype(F32)
             ).astype(BF16)
             copy = pltpu.make_async_copy(
-                outst.at[slot, h], dst.at[h * half : (h + 1) * half], out_sem.at[2 * slot + h]
+                outst.at[slot, h, :, cols],
+                dst.at[h * half : (h + 1) * half, cols],
+                out_sem.at[16 + 4 * slot + 2 * part + h],
             )
             copy.start()
             leaving.append(copy)
@@ -444,26 +470,12 @@
             [buf[4 * h + b, c].reshape(64, buf.shape[-1]) for h, b, c in items], axis=0
         )
 
-    def make_mixed(items, put):
-        def body(n, carry):
-            cols = pl.ds(pl.multiple_of(n * 1024, 1024), 1024)
-            v = nn(rows_of(att, items), wo[:, cols]).reshape(4, 2, 32, 1024)
-            for k in range(4):
-                put(k, cols, v[k])
-            return carry
-
-        lax.fori_loop(0, width // 1024, body, 0)
-
-    def make_gtokens(items, put):
-        def body(n, carry):
-            cols = pl.ds(pl.multiple_of(n * 1024, 1024), 1024)
-            v = nt(rows_of(gq, items), wq[cols, :]) + nn(rows_of(gkv, items), wkv[:, cols])
-            v = v.reshape(4, 2, 32, 1024)
-            for k in range(4):
-                put(k, cols, v[k])
-            return carry
-
-        lax.fori_loop(0, width // 1024, body, 0)
+    def make_mixed(items, cols):
+        return nn(rows_of(att, items), wo[:, cols]).reshape(4, 2, 32, cw)
+
+    def make_gtokens(items, cols):
+        v = nt(rows_of(gq, items), wq[cols, :]) + nn(rows_of(gkv, items), wkv[:, cols])
+        return v.reshape(4, 2, 32, cw)
 
     def keys():
         return kv[:, :, :, :, 0:HEAD].reshape(1024, HEAD)
@@ -615,124 +627,150 @@
 
     work = [
         (ag1, "t", tokens, tok),
+        (ag1, "g", grad_out, grd),
         (wait_local, own_copies[0]),
-        (ag1, "g", grad_out, grd),
         (wait_local, own_copies[1]),
-        (make_mask,),
-        (wait_local, loads[0:6]),
         (ag1b, "t", tok),
-        (wait_local, loads[6:]),
         (ag1b, "g", grd),
         (ag2, "t", tok),
+        (wait_local, loads[0:6]),
+        (project_kv, 0),
         (project, 0),
         (rs_core, "t", pt, xt, 0, 2),
+        (wait_local, loads[6:]),
+        (make_mask,),
         (rs_y1, "t", pt, xt, r1t, 0, 2),
         (ag2b, "t", tok),
         (ag2, "g", grd),
-        (rs_y2, "t", xt, r1t, r2t, 0, 2),
         (project, 1),
         (rs_core, "t", pt, xt, 2, 2),
+        (rs_y2, "t", xt, r1t, r2t, 0, 2),
+        (project_kv, 1),
         (project_grad, 0),
         (rs_core, "g", pg, xg, 0, 2),
         (rs_y1, "t", pt, xt, r1t, 2, 2),
-        (fin_tokens, 0, 2),
         (ag2_end, "t"),
         (project, 2),
+        (rs_y1_low, "g", pg, xg, lowg, r1g, 0, 2),
+        (fin_tokens, 0, 2),
+        (project_kv, 2),
+        (rs_core, "v", pv, xv, 0, 6),
         (rs_core, "t", pt, xt, 4, 2),
-        (rs_y1_low, "g", pg, xg, lowg, r1g, 0, 2),
         (rs_y2, "t", xt, r1t, r2t, 2, 2),
+        (rs_y1, "v", pv, xv, r1v, 0, 6),
+        (rs_y2_low, "g", xg, lowg, r1g, r2g, 0, 2),
         (rs_y1, "t", pt, xt, r1t, 4, 2),
-        (rs_y2_low, "g", xg, lowg, r1g, r2g, 0, 2),
         (ag_end, "t"),
+        (project_kv, 3),
+        (rs_core, "v", pv, xv, 6, 2),
         (project, 3),
         (rs_core, "t", pt, xt, 6, 2),
         (fin_tokens, 2, 2),
-        (rs_y2, "t", xt, r1t, r2t, 4, 2),
+        (rs_y1, "v", pv, xv, r1v, 6, 2),
+        (rs_y2, "v", xv, r1v, r2v, 0, 6),
+        (fin_grads, 0, 2),
         (rs_y1, "t", pt, xt, r1t, 6, 2),
-        (fin_grads, 0, 2),
         (ag2b, "g", grd),
         (project_grad, 1),
+        (rs_y2, "v", xv, r1v, r2v, 6, 2),
         (rs_core, "g", pg, xg, 2, 2),
-        (fin_tokens, 4, 2),
+        (rs_y2, "t", xt, r1t, r2t, 4, 2),
+        (fin_kv, 0, 6),
         (rs_y2, "t", xt, r1t, r2t, 6, 2),
+        (fin_kv, 6, 2),
+        (join_start,),
         (rs_y1_low, "g", pg, xg, lowg, r1g, 2, 2),
         (ag2_end, "g"),
         (project_grad, 2),
         (rs_core, "g", pg, xg, 4, 2),
-        (fin_tokens, 6, 2),
-        (join_start,),
-        (rs_y2_low, "g", xg, lowg, r1g, r2g, 2, 2),
-        (rs_y1_low, "g", pg, xg, lowg, r1g, 4, 2),
+        (fin_tokens, 4, 2),
         (join_end,),
         (agr1, "k", kv, None),
+        (rs_y1_low, "g", pg, xg, lowg, r1g, 4, 2),
+        (fin_tokens, 6, 2),
+        (rs_y2_low, "g", xg, lowg, r1g, r2g, 2, 2),
         (ag_end, "g"),
         (project_grad, 3),
         (rs_core, "g", pg, xg, 6, 2),
+        (agr2, "k", kv, None),
         (rs_y2_low, "g", xg, lowg, r1g, r2g, 4, 2),
         (fin_grads, 2, 2),
-        (agr2, "k", kv, None),
         (rs_y1_low, "g", pg, xg, lowg, r1g, 6, 2),
+        (agr3, "k", kv, None),
         (fin_grads, 4, 2),
-        (agr3, "k", kv, None),
+        (agr_end, "k"),
+        (attend, 1),
         (rs_y2_low, "g", xg, lowg, r1g, r2g, 6, 2),
-        (agr_end, "k"),
         (attend, 0),
-        (attend, 1),
         (agr1, "o0", att, 0),
+        (attend, 3),
+        (attend, 2),
+        (agr1, "o1", att, 1),
         (fin_grads, 6, 2),
-        (attend, 2),
-        (attend, 3),
-        (agr1, "o1", att, 1),
         (attend_back, 0),
+        (attend_back, 1),
         (agr2, "o0", att, 0),
-        (attend_back, 1),
         (attend_back, 2),
-        (agr3, "o0", att, 0),
+        (attend_back, 3),
         (agr2, "o1", att, 1),
-        (attend_back, 3),
-        (agr_end, "o0"),
         (put_dkv,),
-        (rs_core, "d", pd, xd, 0, 8),
-        (agr3, "o1", att, 1),
         (grad_query, 0),
         (agr1, "q0", gq, 0),
+        (agr3, "o0", att, 0),
+        (rs_core, "d", pd, xd, 0, 8),
         (grad_query, 1),
         (agr1, "q1", gq, 1),
+        (agr_end, "o0"),
+        (agr3, "o1", att, 1),
         (rs_y1, "d", pd, xd, r1d, 0, 8),
         (agr_end, "o1"),
-        (rsc_far, "m", make_mixed, f1.at[0]),
-        (rsc_near, "m", make_mixed, f1.at[0], f2.at[0], False),
+        (rsc_far, "m", make_mixed, f1.at[0], 0),
+        (rsc_far, "m", make_mixed, f1.at[0], 1),
+        (rsc_near, "m", make_mixed, f1.at[0], f2.at[0], False, 1),
         (agr2, "q0", gq, 0),
-        (rsc_own, make_mixed),
+        (rsc_own, make_mixed, 1),
+        (rsc_near, "m", make_mixed, f1.at[0], f2.at[0], False, 0),
         (agr2, "q1", gq, 1),
+        (rsc_own, make_mixed, 0),
         (rs_y2, "d", xd, r1d, r2d, 0, 8),
+        (rsc_near, "m", make_mixed, f1.at[0], f2.at[0], True, 0),
         (agr3, "q0", gq, 0),
-        (rsc_near, "m", make_mixed, f1.at[0], f2.at[0], True),
-        (agr_end, "q0"),
         (agr3, "q1", gq, 1),
+        (rsc_near, "m", make_mixed, f1.at[0], f2.at[0], True, 1),
         (grad_w_out, 0),
+        (split_start,),
         (agr_end, "q1"),
+        (grad_w_out, 3),
         (grad_w_out, 1),
-        (split_start,),
-        (grad_w_out, 2),
-        (grad_w_out, 3),
         (split_end,),
         (spread, "w", gkv),
-        (rsc_second, "m", f2.at[0], n1.at[0]),
+        (grad_w_out, 2),
+        (rsc_second, "m", f2.at[0], n1.at[0], 0),
+        (agr_end, "q0"),
+        (rsc_second, "m", f2.at[0], n1.at[0], 1),
+        (rsc_third, "m", n1.at[0], n2.at[0], 0),
         (spread_end, "w"),
-        (rsc_far, "x", make_gtokens, f1.at[1]),
-        (rsc_third, "m", n1.at[0], n2.at[0]),
-        (rsc_near, "x", make_gtokens, f1.at[1], f2.at[1], False),
-        (rsc_near, "x", make_gtokens, f1.at[1], f2.at[1], True),
-        (rsc_last, "m", n2.at[0], mixed, 0),
-        (rsc_own, make_gtokens),
+        (rsc_far, "x", make_gtokens, f1.at[1], 0),
+        (rsc_third, "m", n1.at[0], n2.at[0], 1),
+        (rsc_far, "x", make_gtokens, f1.at[1], 1),
+        (rsc_near, "x", make_gtokens, f1.at[1], f2.at[1], False, 1),
+        (rsc_last, "m", n2.at[0], mixed, 0, 0),
+        (rsc_near, "x", make_gtokens, f1.at[1], f2.at[1], False, 0),
+        (rsc_near, "x", make_gtokens, f1.at[1], f2.at[1], True, 0),
+        (rsc_last, "m", n2.at[0], mixed, 0, 1),
+        (rsc_own, make_gtokens, 1),
+        (rsc_own, make_gtokens, 0),
+        (rsc_near, "x", make_gtokens, f1.at[1], f2.at[1], True, 1),
+        (grad_w_in, 2),
+        (grad_w_in, 1),
         (grad_w_in, 0),
-        (grad_w_in, 1),
-        (grad_w_in, 2),
         (grad_w_in, 3),
-        (rsc_second, "x", f2.at[1], n1.at[1]),
-        (rsc_third, "x", n1.at[1], n2.at[1]),
-        (rsc_last, "x", n2.at[1], gtokens, 1),
+        (rsc_second, "x", f2.at[1], n1.at[1], 0),
+        (rsc_second, "x", f2.at[1], n1.at[1], 1),
+        (rsc_third, "x", n1.at[1], n2.at[1], 0),
+        (rsc_third, "x", n1.at[1], n2.at[1], 1),
+        (rsc_last, "x", n2.at[1], gtokens, 1, 0),
+        (rsc_last, "x", n2.at[1], gtokens, 1, 1),
     ]
     for step in work[:STOP]:
         step[0](*step[1:])
@@ -778,7 +816,7 @@
             pltpu.SemaphoreType.DMA((total,)),
             pltpu.SemaphoreType.DMA((total,)),
         ],
-        compiler_params=pltpu.CompilerParams(vmem_limit_bytes=32 * 2**20),
+        compiler_params=pltpu.CompilerParams(vmem_limit_bytes=VMEM_LIMIT),
     )(*arrays)
 
 
@@ -803,7 +841,8 @@
         vm((width, hn)),
         vm((128, width)),
         vm((hn, width)),
-        *rs_scratch(hn + 128),
+        *rs_scratch(hn),
+        *rs_scratch(128),
         vm((2, CHUNKS, 4, 16, hn), F32),
         vm((CHUNKS, 4, 16, hn), F32),
         vm((CHUNKS, 4, 16, hn)),
@@ -839,7 +878,7 @@
         pltpu.SemaphoreType.DMA((SEMS,)),
         pltpu.SemaphoreType.DMA((SEMS,)),
         pltpu.SemaphoreType.DMA((16,)),
-        pltpu.SemaphoreType.DMA((20,)),
+        pltpu.SemaphoreType.DMA((24,)),
     ]
     anywhere = pl.BlockSpec(memory_space=pl.ANY)
     inside = pl.BlockSpec(memory_space=pltpu.VMEM)

time: 159 us -> 148 us (0.931)
  local copies, waits for them, and re-layouts: 8.17 us -> 0 us
  Pallas kernels: 150 us -> 147 us
    unnamed x12 -> x0, local copies, waits for them, and re-layouts: 8.17 us -> none
    pallas_call x1, Pallas kernels: 145 us -> 140 us  [shards(): pl.pallas_call(kernel, out_shape=(shape((64, width), BF16), shape((64, wi...]
    pallas_call x1, Pallas kernels: 4.58 us -> 7.55 us  [hand_over(): pl.pallas_call(body, out_shape=tuple((jax.ShapeDtypeStruct(a.shape, a.dty...]
where the time goes in v3:
time: 148 us
  Pallas kernels  147 us (99%)
    pallas_call x1, Pallas kernels, shards(): pl.pallas_call(kernel, out_shape=(shape((64, width), BF16), shape((64, wi...  140 us
    pallas_call x1, Pallas kernels, hand_over(): pl.pallas_call(body, out_shape=tuple((jax.ShapeDtypeStruct(a.shape, a.dty...  7.55 us

profile of v3, /device:TPU:0, one launch (start us, length us, event | category | flops | bytes accessed | tf_op | source)
XLA Modules:
  0.0 148.1 jit_solution(13754903714764723673)
XLA Ops:
  0.6 139.7 %shard_map.118 = (bf16[64,2048]{1,0:T(8,128)(2,1)}, bf16[64,2048]{1,0:T(8,128)(2,1)}, bf16[2048,1024]{1,0:T(8,128)(2,1)}, bf16[64,2048]{1,0:T(8,128)(2,1)}, bf16...) custom-call(bf16[64,2048]{1,0:T(8,128)(2,1)} %tokens.1, bf16[64,2048]{1,0:T(8,128)(2,1)} %grad_out.1, ...), custom_call_target="tpu_custom_call" | custom-call | tf_op jit(solution)/shard_map/pallas_call | solution.py:886
  140.3 7.6 %shard_map.119 = (bf16[64,2048]{1,0:T(8,128)(2,1)}, bf16[64,2048]{1,0:T(8,128)(2,1)}, bf16[2048,1024]{1,0:T(8,128)(2,1)}, bf16[64,2048]{1,0:T(8,128)(2,1)}, bf16...) custom-call(bf16[64,2048]{1,0:T(8,128)(2,1)} %get-tuple-element.18.refs_0_, bf16[64,2048]{1,0:T(8,128)(2,1)} %get-tuple-element.19.refs_1_, ...), custom_call_target="tpu_custom_call" | custom-call | tf_op jit(solution)/shard_map/pallas_call | solution.py:809

commit v4 on v3

--- a/solution.py
+++ b/solution.py
@@ -66,7 +66,7 @@
         self.left(*list(self.made))
 
 
-SEMS = 240
+SEMS = 300
 STOP = None
 VMEM_LIMIT = 64 * 2**20
 
@@ -75,7 +75,7 @@
     tokens, grad_out, wq_in, wk_in, wv_in, wo_in, segments,
     mixed, gtokens, gwq, gwk, gwv, gwo,
     tok, grd, wq, wkv, wo,
-    pt, xt, r1t, r2t, pv, xv, r1v, r2v, pg, xg, lowg, r1g, r2g, pd, xd, r1d, r2d,
+    pt, xt, lowt, r1t, r2t, pv, xv, r1v, r2v, rv, pg, xg, lowg, r1g, r2g, pd, xd, lowd, r1d, r2d,
     qr, kvp, kvo, gh, kv, mask, probs, dkt, dvt, dsum, dout, dback, dkeep,
     att, gq, gkv,
     stfar, stnear, own, f1, f2, n1, n2, pfar, pnear, outst,
@@ -134,9 +134,8 @@
         leaving.append(copy)
 
     barrier = pltpu.get_barrier_semaphore()
-    row_peers = [at_core] + [
-        {"row": ring(y, d) * 2 + c} for d in (1, -1, 2) for c in (core, 1 - core)
-    ]
+    row_places = [(1 - core, y)] + [(c, ring(y, d)) for d in (1, -1, 2) for c in (core, 1 - core)]
+    row_peers = [{"row": t * 2 + c} for c, t in row_places]
     peers = [at_x(1), at_x(-1), at_z(1), at_z(-1)] + row_peers
     for device in peers:
         pl.semaphore_signal(barrier, inc=1, device_id=device, device_id_type=MESH)
@@ -151,7 +150,19 @@
         for h in range(2):
             (first, f), (_, s) = axes(h)
             for d in (1, -1):
-                cp.start((name, 1, h, d), src.at[h * half : (h + 1) * half], buf.at[h, s, f], first(d))
+                mine = src.at[h * half : (h + 1) * half]
+                cp.start((name, 1, h, d), mine, buf.at[h, s, f], first(d))
+        for h in range(2):
+            (_, f), (second, s) = axes(h)
+            for d in (1, -1):
+                mine = src.at[h * half : (h + 1) * half]
+                cp.start((name, 3, h, d, 0), mine, buf.at[h, s, f], second(d))
+
+    def ag_second(name, buf, h, k):
+        (_, f), (second, s) = axes(h)
+        for d in (1, -1):
+            part = buf.at[h, s, ring(f, k)]
+            cp.start((name, 3, h, d, k), part, part, second(d))
 
     def ag1b(name, buf):
         for h in range(2):
@@ -160,33 +171,38 @@
             for d, lo in ((1, 0), (-1, 16)):
                 part = buf.at[h, s, ring(f, -d), lo : lo + 16]
                 cp.start((name, 2, h, d), part, part, first(d))
+        for k in (1, -1):
+            for h in range(2):
+                ag_second(name, buf, h, k)
 
     def ag2(name, buf):
         for h in range(2):
             cp.arrived((name, 2, h, 1), (name, 2, h, -1))
-        for first in (True, False):
-            for h in range(2):
-                _, (second, s) = axes(h)
-                for d in (1, -1):
-                    lo = 0 if first == (d == 1) else 2
-                    part = buf.at[h, s, lo : lo + 2]
-                    cp.start((name, 3, h, d, first), part, part, second(d))
+            ag_second(name, buf, h, 2)
+
+    def ag_on(name, buf, d, k):
+        for h in range(2):
+            (_, f), (second, s) = axes(h)
+            cp.arrived((name, 3, h, d, k))
+            part = buf.at[h, ring(s, -d), ring(f, k)]
+            cp.start((name, 4, h, d, k), part, part, second(d))
 
     def ag2b(name, buf):
-        for h in range(2):
-            _, (second, s) = axes(h)
-            cp.arrived((name, 3, h, 1, True), (name, 3, h, -1, True))
-            for d, lo in ((1, 0), (-1, 2)):
-                part = buf.at[h, ring(s, -d), lo : lo + 2]
-                cp.start((name, 4, h, d), part, part, second(d))
+        ag_on(name, buf, 1, 0)
+        ag_on(name, buf, 1, 1)
+        ag_on(name, buf, -1, -1)
+
+    def ag2c(name, buf):
+        ag_on(name, buf, -1, 2)
 
     def ag2_end(name):
         for h in range(2):
-            cp.arrived((name, 3, h, 1, False), (name, 3, h, -1, False))
+            cp.arrived(*[(name, 3, h, d, k) for d in (1, -1) for k in (0, 1, -1, 2)])
 
     def ag_end(name):
         for h in range(2):
-            cp.arrived((name, 4, h, 1), (name, 4, h, -1))
+            cp.arrived(*[(name, 4, h, 1, k) for k in (0, 1)])
+            cp.arrived(*[(name, 4, h, -1, k) for k in (-1, 2)])
 
     steps = ((0, 0), (-1, 1), (1, -1), (2, 2))
     pairs = [(ring(z, s), ring(x, s)) for s in (0, 1, -1, 2)]
@@ -297,6 +313,18 @@
         rs_wait("t", s0)
         for s in range(s0, s0 + n):
             qr[chunk_of(s)] = rs_value(xt, r2t, s).astype(BF16)
+
+    def send_kv():
+        for n, ((c, t), device) in enumerate(zip(row_places, row_peers)):
+            cp.start(("v", n), pv.at[c, 6:8, t], rv.at[n], device)
+
+    def fin_kv_late():
+        cp.arrived(*[("v", n) for n in range(len(row_peers))])
+        for s in range(2):
+            total = pv[core, 6 + s, y]
+            for n in range(len(row_peers)):
+                total = total + rv[n, s]
+            kvp[chunk_of(6 + s)] = total.astype(BF16)
 
     def fin_kv(s0, n):
         rs_wait("v", s0)
@@ -627,150 +655,150 @@
 
     work = [
         (ag1, "t", tokens, tok),
-        (ag1, "g", grad_out, grd),
         (wait_local, own_copies[0]),
-        (wait_local, own_copies[1]),
         (ag1b, "t", tok),
-        (ag1b, "g", grd),
         (ag2, "t", tok),
         (wait_local, loads[0:6]),
-        (project_kv, 0),
         (project, 0),
         (rs_core, "t", pt, xt, 0, 2),
+        (project_kv, 0),
         (wait_local, loads[6:]),
         (make_mask,),
-        (rs_y1, "t", pt, xt, r1t, 0, 2),
+        (rs_y1_low, "t", pt, xt, lowt, r1t, 0, 2),
         (ag2b, "t", tok),
+        (rs_y2_low, "t", xt, lowt, r1t, r2t, 0, 2),
+        (ag2c, "t", tok),
+        (ag1, "g", grad_out, grd),
+        (wait_local, own_copies[1]),
+        (ag2_end, "t"),
+        (project_kv, 2),
+        (project_kv, 1),
+        (rs_core, "v", pv, xv, 0, 6),
+        (project, 2),
+        (rs_core, "t", pt, xt, 4, 2),
+        (project, 1),
+        (rs_y1, "v", pv, xv, r1v, 0, 6),
+        (fin_tokens, 0, 2),
+        (rs_core, "t", pt, xt, 2, 2),
+        (ag_end, "t"),
+        (project_kv, 3),
+        (send_kv,),
+        (project, 3),
+        (rs_core, "t", pt, xt, 6, 2),
+        (rs_y1_low, "t", pt, xt, lowt, r1t, 2, 2),
+        (ag1b, "g", grd),
+        (rs_y1_low, "t", pt, xt, lowt, r1t, 4, 2),
+        (rs_y2, "v", xv, r1v, r2v, 0, 6),
+        (rs_y1_low, "t", pt, xt, lowt, r1t, 6, 2),
+        (fin_kv_late,),
+        (rs_y2_low, "t", xt, lowt, r1t, r2t, 2, 2),
+        (rs_y2_low, "t", xt, lowt, r1t, r2t, 4, 2),
         (ag2, "g", grd),
-        (project, 1),
-        (rs_core, "t", pt, xt, 2, 2),
-        (rs_y2, "t", xt, r1t, r2t, 0, 2),
-        (project_kv, 1),
         (project_grad, 0),
         (rs_core, "g", pg, xg, 0, 2),
-        (rs_y1, "t", pt, xt, r1t, 2, 2),
-        (ag2_end, "t"),
-        (project, 2),
+        (rs_y2_low, "t", xt, lowt, r1t, r2t, 6, 2),
+        (fin_kv, 0, 6),
+        (join_start,),
+        (fin_tokens, 2, 2),
+        (fin_tokens, 4, 2),
         (rs_y1_low, "g", pg, xg, lowg, r1g, 0, 2),
-        (fin_tokens, 0, 2),
-        (project_kv, 2),
-        (rs_core, "v", pv, xv, 0, 6),
-        (rs_core, "t", pt, xt, 4, 2),
-        (rs_y2, "t", xt, r1t, r2t, 2, 2),
-        (rs_y1, "v", pv, xv, r1v, 0, 6),
+        (join_end,),
+        (ag2b, "g", grd),
+        (fin_tokens, 6, 2),
+        (agr1, "k", kv, None),
         (rs_y2_low, "g", xg, lowg, r1g, r2g, 0, 2),
-        (rs_y1, "t", pt, xt, r1t, 4, 2),
-        (ag_end, "t"),
-        (project_kv, 3),
-        (rs_core, "v", pv, xv, 6, 2),
-        (project, 3),
-        (rs_core, "t", pt, xt, 6, 2),
-        (fin_tokens, 2, 2),
-        (rs_y1, "v", pv, xv, r1v, 6, 2),
-        (rs_y2, "v", xv, r1v, r2v, 0, 6),
+        (ag2_end, "g"),
+        (ag2c, "g", grd),
+        (project_grad, 1),
+        (rs_core, "g", pg, xg, 2, 2),
+        (agr2, "k", kv, None),
+        (project_grad, 2),
         (fin_grads, 0, 2),
-        (rs_y1, "t", pt, xt, r1t, 6, 2),
-        (ag2b, "g", grd),
-        (project_grad, 1),
-        (rs_y2, "v", xv, r1v, r2v, 6, 2),
-        (rs_core, "g", pg, xg, 2, 2),
-        (rs_y2, "t", xt, r1t, r2t, 4, 2),
-        (fin_kv, 0, 6),
-        (rs_y2, "t", xt, r1t, r2t, 6, 2),
-        (fin_kv, 6, 2),
-        (join_start,),
+        (rs_core, "g", pg, xg, 4, 2),
         (rs_y1_low, "g", pg, xg, lowg, r1g, 2, 2),
-        (ag2_end, "g"),
-        (project_grad, 2),
-        (rs_core, "g", pg, xg, 4, 2),
-        (fin_tokens, 4, 2),
-        (join_end,),
-        (agr1, "k", kv, None),
-        (rs_y1_low, "g", pg, xg, lowg, r1g, 4, 2),
-        (fin_tokens, 6, 2),
-        (rs_y2_low, "g", xg, lowg, r1g, r2g, 2, 2),
+        (agr3, "k", kv, None),
         (ag_end, "g"),
         (project_grad, 3),
+        (rs_y1_low, "g", pg, xg, lowg, r1g, 4, 2),
+        (agr_end, "k"),
         (rs_core, "g", pg, xg, 6, 2),
-        (agr2, "k", kv, None),
+        (attend, 0),
+        (rs_y2_low, "g", xg, lowg, r1g, r2g, 2, 2),
+        (attend, 2),
         (rs_y2_low, "g", xg, lowg, r1g, r2g, 4, 2),
+        (rs_y1_low, "g", pg, xg, lowg, r1g, 6, 2),
+        (attend, 3),
+        (agr1, "o1", att, 1),
+        (attend, 1),
         (fin_grads, 2, 2),
-        (rs_y1_low, "g", pg, xg, lowg, r1g, 6, 2),
-        (agr3, "k", kv, None),
+        (agr1, "o0", att, 0),
         (fin_grads, 4, 2),
-        (agr_end, "k"),
-        (attend, 1),
         (rs_y2_low, "g", xg, lowg, r1g, r2g, 6, 2),
-        (attend, 0),
-        (agr1, "o0", att, 0),
-        (attend, 3),
-        (attend, 2),
-        (agr1, "o1", att, 1),
+        (agr2, "o1", att, 1),
+        (agr2, "o0", att, 0),
         (fin_grads, 6, 2),
         (attend_back, 0),
+        (agr3, "o1", att, 1),
         (attend_back, 1),
-        (agr2, "o0", att, 0),
+        (agr3, "o0", att, 0),
         (attend_back, 2),
+        (agr_end, "o1"),
         (attend_back, 3),
-        (agr2, "o1", att, 1),
         (put_dkv,),
+        (rs_core, "d", pd, xd, 0, 8),
+        (agr_end, "o0"),
+        (rsc_far, "m", make_mixed, f1.at[0], 1),
         (grad_query, 0),
+        (rsc_far, "m", make_mixed, f1.at[0], 0),
+        (rsc_near, "m", make_mixed, f1.at[0], f2.at[0], False, 0),
+        (rs_y1_low, "d", pd, xd, lowd, r1d, 0, 8),
+        (rsc_own, make_mixed, 0),
         (agr1, "q0", gq, 0),
-        (agr3, "o0", att, 0),
-        (rs_core, "d", pd, xd, 0, 8),
+        (rsc_near, "m", make_mixed, f1.at[0], f2.at[0], False, 1),
+        (rsc_own, make_mixed, 1),
         (grad_query, 1),
+        (rs_y2_low, "d", xd, lowd, r1d, r2d, 0, 8),
+        (rsc_near, "m", make_mixed, f1.at[0], f2.at[0], True, 1),
         (agr1, "q1", gq, 1),
-        (agr_end, "o0"),
-        (agr3, "o1", att, 1),
-        (rs_y1, "d", pd, xd, r1d, 0, 8),
-        (agr_end, "o1"),
-        (rsc_far, "m", make_mixed, f1.at[0], 0),
-        (rsc_far, "m", make_mixed, f1.at[0], 1),
-        (rsc_near, "m", make_mixed, f1.at[0], f2.at[0], False, 1),
+        (rsc_near, "m", make_mixed, f1.at[0], f2.at[0], True, 0),
         (agr2, "q0", gq, 0),
-        (rsc_own, make_mixed, 1),
-        (rsc_near, "m", make_mixed, f1.at[0], f2.at[0], False, 0),
-        (agr2, "q1", gq, 1),
-        (rsc_own, make_mixed, 0),
-        (rs_y2, "d", xd, r1d, r2d, 0, 8),
-        (rsc_near, "m", make_mixed, f1.at[0], f2.at[0], True, 0),
-        (agr3, "q0", gq, 0),
-        (agr3, "q1", gq, 1),
-        (rsc_near, "m", make_mixed, f1.at[0], f2.at[0], True, 1),
         (grad_w_out, 0),
         (split_start,),
-        (agr_end, "q1"),
-        (grad_w_out, 3),
         (grad_w_out, 1),
+        (agr2, "q1", gq, 1),
         (split_end,),
         (spread, "w", gkv),
+        (agr3, "q0", gq, 0),
+        (grad_w_out, 3),
+        (rsc_second, "m", f2.at[0], n1.at[0], 1),
+        (agr3, "q1", gq, 1),
+        (agr_end, "q0"),
         (grad_w_out, 2),
         (rsc_second, "m", f2.at[0], n1.at[0], 0),
-        (agr_end, "q0"),
-        (rsc_second, "m", f2.at[0], n1.at[0], 1),
+        (agr_end, "q1"),
+        (rsc_third, "m", n1.at[0], n2.at[0], 1),
+        (spread_end, "w"),
+        (rsc_far, "x", make_gtokens, f1.at[1], 1),
+        (rsc_far, "x", make_gtokens, f1.at[1], 0),
         (rsc_third, "m", n1.at[0], n2.at[0], 0),
-        (spread_end, "w"),
-        (rsc_far, "x", make_gtokens, f1.at[1], 0),
-        (rsc_third, "m", n1.at[0], n2.at[0], 1),
-        (rsc_far, "x", make_gtokens, f1.at[1], 1),
         (rsc_near, "x", make_gtokens, f1.at[1], f2.at[1], False, 1),
+        (rsc_near, "x", make_gtokens, f1.at[1], f2.at[1], False, 0),
+        (rsc_last, "m", n2.at[0], mixed, 0, 1),
+        (rsc_near, "x", make_gtokens, f1.at[1], f2.at[1], True, 1),
+        (rsc_near, "x", make_gtokens, f1.at[1], f2.at[1], True, 0),
         (rsc_last, "m", n2.at[0], mixed, 0, 0),
-        (rsc_near, "x", make_gtokens, f1.at[1], f2.at[1], False, 0),
-        (rsc_near, "x", make_gtokens, f1.at[1], f2.at[1], True, 0),
-        (rsc_last, "m", n2.at[0], mixed, 0, 1),
         (rsc_own, make_gtokens, 1),
         (rsc_own, make_gtokens, 0),
-        (rsc_near, "x", make_gtokens, f1.at[1], f2.at[1], True, 1),
         (grad_w_in, 2),
         (grad_w_in, 1),
         (grad_w_in, 0),
+        (rsc_second, "x", f2.at[1], n1.at[1], 1),
         (grad_w_in, 3),
         (rsc_second, "x", f2.at[1], n1.at[1], 0),
-        (rsc_second, "x", f2.at[1], n1.at[1], 1),
+        (rsc_third, "x", n1.at[1], n2.at[1], 1),
         (rsc_third, "x", n1.at[1], n2.at[1], 0),
-        (rsc_third, "x", n1.at[1], n2.at[1], 1),
+        (rsc_last, "x", n2.at[1], gtokens, 1, 1),
         (rsc_last, "x", n2.at[1], gtokens, 1, 0),
-        (rsc_last, "x", n2.at[1], gtokens, 1, 1),
     ]
     for step in work[:STOP]:
         step[0](*step[1:])
@@ -841,14 +869,23 @@
         vm((width, hn)),
         vm((128, width)),
         vm((hn, width)),
-        *rs_scratch(hn),
-        *rs_scratch(128),
         vm((2, CHUNKS, 4, 16, hn), F32),
         vm((CHUNKS, 4, 16, hn), F32),
         vm((CHUNKS, 4, 16, hn)),
         vm((2, CHUNKS, 16, hn // 2)),
         vm((2, CHUNKS, 16, hn)),
-        *rs_scratch(2 * HEAD),
+        *rs_scratch(128),
+        vm((7, 2, 16, 128), F32),
+        vm((2, CHUNKS, 4, 16, hn), F32),
+        vm((CHUNKS, 4, 16, hn), F32),
+        vm((CHUNKS, 4, 16, hn)),
+        vm((2, CHUNKS, 16, hn // 2)),
+        vm((2, CHUNKS, 16, hn)),
+        vm((2, CHUNKS, 4, 16, 2 * HEAD), F32),
+        vm((CHUNKS, 4, 16, 2 * HEAD), F32),
+        vm((CHUNKS, 4, 16, 2 * HEAD)),
+        vm((2, CHUNKS, 16, HEAD)),
+        vm((2, CHUNKS, 16, 2 * HEAD)),
         vm((CHUNKS, 16, hn)),
         vm((CHUNKS, 16, 128)),
         vm((CHUNKS, 16, 128)),

time: 148 us -> 146 us (0.986)
    pallas_call x1, Pallas kernels: 140 us -> 138 us  [shards(): pl.pallas_call(kernel, out_shape=(shape((64, width), BF16), shape((64, wi...]
where the time goes in v4:
time: 146 us
  Pallas kernels  146 us (100%)
    pallas_call x1, Pallas kernels, shards(): pl.pallas_call(kernel, out_shape=(shape((64, width), BF16), shape((64, wi...  138 us
    pallas_call x1, Pallas kernels, hand_over(): pl.pallas_call(body, out_shape=tuple((jax.ShapeDtypeStruct(a.shape, a.dty...  7.55 us

profile of v4, /device:TPU:0, one launch (start us, length us, event | category | flops | bytes accessed | tf_op | source)
XLA Modules:
  0.0 146.3 jit_solution(5709917872103314053)
XLA Ops:
  0.6 138.0 %shard_map.118 = (bf16[64,2048]{1,0:T(8,128)(2,1)}, bf16[64,2048]{1,0:T(8,128)(2,1)}, bf16[2048,1024]{1,0:T(8,128)(2,1)}, bf16[64,2048]{1,0:T(8,128)(2,1)}, bf16...) custom-call(bf16[64,2048]{1,0:T(8,128)(2,1)} %tokens.1, bf16[64,2048]{1,0:T(8,128)(2,1)} %grad_out.1, ...), custom_call_target="tpu_custom_call" | custom-call | tf_op jit(solution)/shard_map/pallas_call | solution.py:923
  138.6 7.6 %shard_map.119 = (bf16[64,2048]{1,0:T(8,128)(2,1)}, bf16[64,2048]{1,0:T(8,128)(2,1)}, bf16[2048,1024]{1,0:T(8,128)(2,1)}, bf16[64,2048]{1,0:T(8,128)(2,1)}, bf16...) custom-call(bf16[64,2048]{1,0:T(8,128)(2,1)} %get-tuple-element.18.refs_0_, bf16[64,2048]{1,0:T(8,128)(2,1)} %get-tuple-element.19.refs_1_, ...), custom_call_target="tpu_custom_call" | custom-call | tf_op jit(solution)/shard_map/pallas_call | solution.py:837

commit v5 on v4

--- a/solution.py
+++ b/solution.py
@@ -75,7 +75,7 @@
     tokens, grad_out, wq_in, wk_in, wv_in, wo_in, segments,
     mixed, gtokens, gwq, gwk, gwv, gwo,
     tok, grd, wq, wkv, wo,
-    pt, xt, lowt, r1t, r2t, pv, xv, r1v, r2v, rv, pg, xg, lowg, r1g, r2g, pd, xd, lowd, r1d, r2d,
+    pt, xt, r1t, r2t, pv, xv, r1v, r2v, rv, pg, xg, lowg, r1g, r2g, pd, xd, lowd, r1d, r2d,
     qr, kvp, kvo, gh, kv, mask, probs, dkt, dvt, dsum, dout, dback, dkeep,
     att, gq, gkv,
     stfar, stnear, own, f1, f2, n1, n2, pfar, pnear, outst,
@@ -129,9 +129,11 @@
         for copy in pair:
             copy.start()
             leaving.append(copy)
-    for copy in loads:
-        copy.start()
-        leaving.append(copy)
+
+    def start_local(copies):
+        for copy in copies:
+            copy.start()
+            leaving.append(copy)
 
     barrier = pltpu.get_barrier_semaphore()
     row_places = [(1 - core, y)] + [(c, ring(y, d)) for d in (1, -1, 2) for c in (core, 1 - core)]
@@ -655,134 +657,136 @@
 
     work = [
         (ag1, "t", tokens, tok),
+        (start_local, loads[0:6]),
         (wait_local, own_copies[0]),
         (ag1b, "t", tok),
         (ag2, "t", tok),
         (wait_local, loads[0:6]),
+        (start_local, loads[6:]),
         (project, 0),
         (rs_core, "t", pt, xt, 0, 2),
         (project_kv, 0),
+        (make_mask,),
+        (rs_y1, "t", pt, xt, r1t, 0, 2),
+        (ag2b, "t", tok),
         (wait_local, loads[6:]),
-        (make_mask,),
-        (rs_y1_low, "t", pt, xt, lowt, r1t, 0, 2),
-        (ag2b, "t", tok),
-        (rs_y2_low, "t", xt, lowt, r1t, r2t, 0, 2),
         (ag2c, "t", tok),
-        (ag1, "g", grad_out, grd),
-        (wait_local, own_copies[1]),
         (ag2_end, "t"),
         (project_kv, 2),
+        (ag1, "g", grad_out, grd),
         (project_kv, 1),
         (rs_core, "v", pv, xv, 0, 6),
         (project, 2),
         (rs_core, "t", pt, xt, 4, 2),
+        (rs_y2, "t", xt, r1t, r2t, 0, 2),
         (project, 1),
         (rs_y1, "v", pv, xv, r1v, 0, 6),
-        (fin_tokens, 0, 2),
         (rs_core, "t", pt, xt, 2, 2),
         (ag_end, "t"),
         (project_kv, 3),
+        (rs_y1, "t", pt, xt, r1t, 4, 2),
         (send_kv,),
         (project, 3),
+        (ag1b, "g", grd),
         (rs_core, "t", pt, xt, 6, 2),
-        (rs_y1_low, "t", pt, xt, lowt, r1t, 2, 2),
-        (ag1b, "g", grd),
-        (rs_y1_low, "t", pt, xt, lowt, r1t, 4, 2),
         (rs_y2, "v", xv, r1v, r2v, 0, 6),
-        (rs_y1_low, "t", pt, xt, lowt, r1t, 6, 2),
+        (fin_tokens, 0, 2),
+        (rs_y1, "t", pt, xt, r1t, 2, 2),
+        (wait_local, own_copies[1]),
+        (rs_y2, "t", xt, r1t, r2t, 4, 2),
+        (rs_y1, "t", pt, xt, r1t, 6, 2),
         (fin_kv_late,),
-        (rs_y2_low, "t", xt, lowt, r1t, r2t, 2, 2),
-        (rs_y2_low, "t", xt, lowt, r1t, r2t, 4, 2),
         (ag2, "g", grd),
         (project_grad, 0),
-        (rs_core, "g", pg, xg, 0, 2),
-        (rs_y2_low, "t", xt, lowt, r1t, r2t, 6, 2),
         (fin_kv, 0, 6),
         (join_start,),
-        (fin_tokens, 2, 2),
+        (rs_y2, "t", xt, r1t, r2t, 2, 2),
+        (rs_core, "g", pg, xg, 0, 2),
         (fin_tokens, 4, 2),
-        (rs_y1_low, "g", pg, xg, lowg, r1g, 0, 2),
         (join_end,),
         (ag2b, "g", grd),
-        (fin_tokens, 6, 2),
         (agr1, "k", kv, None),
-        (rs_y2_low, "g", xg, lowg, r1g, r2g, 0, 2),
+        (rs_y1_low, "g", pg, xg, lowg, r1g, 0, 2),
+        (rs_y2, "t", xt, r1t, r2t, 6, 2),
+        (ag2c, "g", grd),
         (ag2_end, "g"),
-        (ag2c, "g", grd),
         (project_grad, 1),
         (rs_core, "g", pg, xg, 2, 2),
+        (fin_tokens, 2, 2),
         (agr2, "k", kv, None),
         (project_grad, 2),
-        (fin_grads, 0, 2),
+        (rs_y2_low, "g", xg, lowg, r1g, r2g, 0, 2),
         (rs_core, "g", pg, xg, 4, 2),
         (rs_y1_low, "g", pg, xg, lowg, r1g, 2, 2),
-        (agr3, "k", kv, None),
         (ag_end, "g"),
         (project_grad, 3),
+        (agr3, "k", kv, None),
         (rs_y1_low, "g", pg, xg, lowg, r1g, 4, 2),
+        (rs_core, "g", pg, xg, 6, 2),
+        (fin_grads, 0, 2),
+        (fin_tokens, 6, 2),
+        (rs_y2_low, "g", xg, lowg, r1g, r2g, 2, 2),
         (agr_end, "k"),
-        (rs_core, "g", pg, xg, 6, 2),
-        (attend, 0),
-        (rs_y2_low, "g", xg, lowg, r1g, r2g, 2, 2),
-        (attend, 2),
+        (attend, 1),
         (rs_y2_low, "g", xg, lowg, r1g, r2g, 4, 2),
         (rs_y1_low, "g", pg, xg, lowg, r1g, 6, 2),
+        (attend, 0),
+        (agr1, "o0", att, 0),
+        (attend, 2),
         (attend, 3),
+        (rs_y2_low, "g", xg, lowg, r1g, r2g, 6, 2),
         (agr1, "o1", att, 1),
-        (attend, 1),
+        (fin_grads, 4, 2),
         (fin_grads, 2, 2),
-        (agr1, "o0", att, 0),
-        (fin_grads, 4, 2),
-        (rs_y2_low, "g", xg, lowg, r1g, r2g, 6, 2),
-        (agr2, "o1", att, 1),
         (agr2, "o0", att, 0),
         (fin_grads, 6, 2),
         (attend_back, 0),
-        (agr3, "o1", att, 1),
         (attend_back, 1),
+        (agr2, "o1", att, 1),
+        (attend_back, 2),
         (agr3, "o0", att, 0),
-        (attend_back, 2),
-        (agr_end, "o1"),
         (attend_back, 3),
         (put_dkv,),
         (rs_core, "d", pd, xd, 0, 8),
+        (grad_query, 1),
+        (agr3, "o1", att, 1),
         (agr_end, "o0"),
+        (grad_query, 0),
+        (rs_y1_low, "d", pd, xd, lowd, r1d, 0, 8),
+        (agr_end, "o1"),
         (rsc_far, "m", make_mixed, f1.at[0], 1),
-        (grad_query, 0),
+        (agr1, "q1", gq, 1),
+        (agr1, "q0", gq, 0),
         (rsc_far, "m", make_mixed, f1.at[0], 0),
-        (rsc_near, "m", make_mixed, f1.at[0], f2.at[0], False, 0),
-        (rs_y1_low, "d", pd, xd, lowd, r1d, 0, 8),
-        (rsc_own, make_mixed, 0),
-        (agr1, "q0", gq, 0),
         (rsc_near, "m", make_mixed, f1.at[0], f2.at[0], False, 1),
         (rsc_own, make_mixed, 1),
-        (grad_query, 1),
         (rs_y2_low, "d", xd, lowd, r1d, r2d, 0, 8),
+        (rsc_near, "m", make_mixed, f1.at[0], f2.at[0], False, 0),
+        (rsc_own, make_mixed, 0),
         (rsc_near, "m", make_mixed, f1.at[0], f2.at[0], True, 1),
-        (agr1, "q1", gq, 1),
+        (agr2, "q1", gq, 1),
         (rsc_near, "m", make_mixed, f1.at[0], f2.at[0], True, 0),
         (agr2, "q0", gq, 0),
+        (grad_w_out, 1),
+        (split_start,),
+        (agr3, "q1", gq, 1),
         (grad_w_out, 0),
-        (split_start,),
-        (grad_w_out, 1),
-        (agr2, "q1", gq, 1),
+        (agr3, "q0", gq, 0),
+        (agr_end, "q1"),
         (split_end,),
         (spread, "w", gkv),
-        (agr3, "q0", gq, 0),
+        (grad_w_out, 2),
+        (agr_end, "q0"),
+        (rsc_second, "m", f2.at[0], n1.at[0], 1),
         (grad_w_out, 3),
-        (rsc_second, "m", f2.at[0], n1.at[0], 1),
-        (agr3, "q1", gq, 1),
-        (agr_end, "q0"),
-        (grad_w_out, 2),
         (rsc_second, "m", f2.at[0], n1.at[0], 0),
-        (agr_end, "q1"),
         (rsc_third, "m", n1.at[0], n2.at[0], 1),
         (spread_end, "w"),
         (rsc_far, "x", make_gtokens, f1.at[1], 1),
         (rsc_far, "x", make_gtokens, f1.at[1], 0),
         (rsc_third, "m", n1.at[0], n2.at[0], 0),
+        (rsc_near, "x", make_gtokens, f1.at[1], f2.at[1], False, 0),
         (rsc_near, "x", make_gtokens, f1.at[1], f2.at[1], False, 1),
-        (rsc_near, "x", make_gtokens, f1.at[1], f2.at[1], False, 0),
         (rsc_last, "m", n2.at[0], mixed, 0, 1),
         (rsc_near, "x", make_gtokens, f1.at[1], f2.at[1], True, 1),
         (rsc_near, "x", make_gtokens, f1.at[1], f2.at[1], True, 0),
@@ -869,11 +873,7 @@
         vm((width, hn)),
         vm((128, width)),
         vm((hn, width)),
-        vm((2, CHUNKS, 4, 16, hn), F32),
-        vm((CHUNKS, 4, 16, hn), F32),
-        vm((CHUNKS, 4, 16, hn)),
-        vm((2, CHUNKS, 16, hn // 2)),
-        vm((2, CHUNKS, 16, hn)),
+        *rs_scratch(hn),
         *rs_scratch(128),
         vm((7, 2, 16, 128), F32),
         vm((2, CHUNKS, 4, 16, hn), F32),

time: 146 us -> 147 us (level)
  no operation moved by 1% of the time
where the time goes in v5:
time: 147 us
  Pallas kernels  146 us (99%)
    pallas_call x1, Pallas kernels, shards(): pl.pallas_call(kernel, out_shape=(shape((64, width), BF16), shape((64, wi...  138 us
    pallas_call x1, Pallas kernels, hand_over(): pl.pallas_call(body, out_shape=tuple((jax.ShapeDtypeStruct(a.shape, a.dty...  7.55 us

profile of v5, /device:TPU:0, one launch (start us, length us, event | category | flops | bytes accessed | tf_op | source)
XLA Modules:
  0.0 146.6 jit_solution(1325272937125222307)
XLA Ops:
  0.6 138.2 %shard_map.118 = (bf16[64,2048]{1,0:T(8,128)(2,1)}, bf16[64,2048]{1,0:T(8,128)(2,1)}, bf16[2048,1024]{1,0:T(8,128)(2,1)}, bf16[64,2048]{1,0:T(8,128)(2,1)}, bf16...) custom-call(bf16[64,2048]{1,0:T(8,128)(2,1)} %tokens.1, bf16[64,2048]{1,0:T(8,128)(2,1)} %grad_out.1, ...), custom_call_target="tpu_custom_call" | custom-call | tf_op jit(solution)/shard_map/pallas_call | solution.py:923
  138.8 7.6 %shard_map.119 = (bf16[64,2048]{1,0:T(8,128)(2,1)}, bf16[64,2048]{1,0:T(8,128)(2,1)}, bf16[2048,1024]{1,0:T(8,128)(2,1)}, bf16[64,2048]{1,0:T(8,128)(2,1)}, bf16...) custom-call(bf16[64,2048]{1,0:T(8,128)(2,1)} %get-tuple-element.18.refs_0_, bf16[64,2048]{1,0:T(8,128)(2,1)} %get-tuple-element.19.refs_1_, ...), custom_call_target="tpu_custom_call" | custom-call | tf_op jit(solution)/shard_map/pallas_call | solution.py:841
